TPU v7x, 32 devices: a whole 2x2x4 slice. The times are simulated.
32 devices in a mesh: seq: 16 (over z, y, core), head: 2 (over x).
Axes of the slice: x: 2, y: 2, z: 4, core: 2. Of those that a mesh axis runs over, the one named last changes fastest.
Arguments:
- queries: bfloat16 [192, 64, 128], P('seq', 'head'), may hold values from -88 to 88
- prompt_keys: bfloat16 [32768, 8, 128], P('seq', 'head'), may hold values from -4 to 4
- prompt_values: bfloat16 [32768, 8, 128], P('seq', 'head'), may hold values from -6 to 6
- suffix_keys: bfloat16 [192, 8, 1024, 128], P('seq', 'head'), may hold values from -8 to 8
- suffix_values: bfloat16 [192, 8, 1024, 128], P('seq', 'head'), may hold values from -6 to 6
- suffix_lengths: int32 [192], P('seq'), may hold values from 1 to 1024, as said below
- slot_of_sample: int32 [192], replicated, may hold values from 0 to 191, each once
- out_weight: bfloat16 [8192, 5120], P('head', 'seq'), may hold values from -0.0625 to 0.0625
Outputs:
- projected: float32 [192, 5120], P('head', 'seq')
Inputs may be any that keep to these rules, and one draw needn't show every extreme that they name: `suffix_lengths`: slot j is held with the samples of seq index j // 12; some slot has exactly 1024 live tokens. `slot_of_sample`: each slot is named once.
All inputs are finite; a program needn't handle non-finite values.
Results may differ from a plain program's by a relative error of at most 0.006.
Values may be sent and summed in bfloat16 or wider, within the bound.
A program may use at most 128 MiB of HBM per device.

v0:
```python
import math

import jax
import jax.numpy as jnp
from jax import lax
from jax.sharding import PartitionSpec as P


def partial_softmax(scores, values_block, equation):
    row_max = jnp.max(scores, axis=-1)
    weights = jnp.exp(scores - row_max[..., None])
    row_total = jnp.sum(weights, axis=-1)
    output = jnp.einsum(
        equation, weights.astype(jnp.bfloat16), values_block, preferred_element_type=jnp.float32
    )
    return (output, row_max, row_total)


def per_device(
    queries,
    prompt_keys,
    prompt_values,
    suffix_keys,
    suffix_values,
    suffix_lengths,
    slot_of_sample,
    out_weight,
):
    local_count, heads_local, head_width = queries.shape
    kv_local = prompt_keys.shape[1]
    group_size = heads_local // kv_local
    score_scale = 1.0 / math.sqrt(head_width)
    all_queries = lax.all_gather(queries, "seq", axis=0, tiled=True)
    total_rows = all_queries.shape[0]
    block_rows = math.gcd(total_rows, 64)

    def prefix_block(query_block):
        grouped = query_block.reshape(block_rows, kv_local, group_size, head_width)
        scores = (
            jnp.einsum("bkgd,pkd->bkgp", grouped, prompt_keys, preferred_element_type=jnp.float32)
            * score_scale
        )
        output, row_max, row_total = partial_softmax(scores, prompt_values, "bkgp,pkd->bkgd")
        return (
            output.reshape(block_rows, heads_local, head_width),
            row_max.reshape(block_rows, heads_local),
            row_total.reshape(block_rows, heads_local),
        )

    blocks = all_queries.reshape(total_rows // block_rows, block_rows, heads_local, head_width)
    pre_out, pre_max, pre_total = lax.map(prefix_block, blocks)
    pre_out = pre_out.reshape(total_rows, heads_local, head_width)
    pre_max = pre_max.reshape(total_rows, heads_local)
    pre_total = pre_total.reshape(total_rows, heads_local)
    my_slots = lax.axis_index("seq") * local_count + jnp.arange(local_count, dtype=jnp.int32)
    matches = (slot_of_sample[None, :] == my_slots[:, None]).astype(jnp.int32)
    samples = jnp.sum(matches * jnp.arange(total_rows, dtype=jnp.int32)[None, :], axis=1)
    own_queries = all_queries[samples].reshape(local_count, kv_local, group_size, head_width)
    tail_scores = (
        jnp.einsum("bkgd,bksd->bkgs", own_queries, suffix_keys, preferred_element_type=jnp.float32)
        * score_scale
    )
    positions = jnp.arange(suffix_keys.shape[2], dtype=jnp.int32)
    live_mask = positions[None, None, None, :] < suffix_lengths[:, None, None, None]
    tail_scores = jnp.where(live_mask, tail_scores, jnp.float32(-1e30))
    tail_out, tail_max, tail_total = partial_softmax(tail_scores, suffix_values, "bkgs,bksd->bkgd")
    tail_out = tail_out.reshape(local_count, heads_local, head_width)
    tail_max = tail_max.reshape(local_count, heads_local)
    tail_total = tail_total.reshape(local_count, heads_local)
    old_max = pre_max[samples]
    joint_max = jnp.maximum(old_max, tail_max)
    old_factor = jnp.exp(old_max - joint_max)
    new_factor = jnp.exp(tail_max - joint_max)
    joint_out = pre_out[samples] * old_factor[..., None] + tail_out * new_factor[..., None]
    joint_total = pre_total[samples] * old_factor + tail_total * new_factor
    pre_out = pre_out.at[samples].set(joint_out)
    pre_max = pre_max.at[samples].set(joint_max)
    pre_total = pre_total.at[samples].set(joint_total)
    got_out, got_max, got_total = (
        lax.all_to_all(pre_out[None], "seq", split_axis=1, concat_axis=0, tiled=True),
        lax.all_to_all(pre_max[None], "seq", split_axis=1, concat_axis=0, tiled=True),
        lax.all_to_all(pre_total[None], "seq", split_axis=1, concat_axis=0, tiled=True),
    )
    best = jnp.max(got_max, axis=0)
    factors = jnp.exp(got_max - best[None])
    merged_out = jnp.sum(got_out * factors[..., None], axis=0)
    merged_total = jnp.sum(got_total * factors, axis=0)
    attention = (merged_out / merged_total[..., None]).astype(jnp.bfloat16)
    attention = attention.reshape(local_count, heads_local * head_width)
    terms = jnp.dot(
        lax.all_gather(attention, "seq", axis=0, tiled=True),
        out_weight,
        preferred_element_type=jnp.float32,
    )
    return lax.psum_scatter(terms, "head", scatter_dimension=0, tiled=True)


def solution(mesh):
    placed = (
        P("seq", "head", None),
        P("seq", "head", None),
        P("seq", "head", None),
        P("seq", "head", None, None),
        P("seq", "head", None, None),
        P("seq"),
        P(),
        P("head", "seq"),
    )
    return jax.shard_map(
        per_device, mesh=mesh, in_specs=placed, out_specs=P("head", "seq"), check_vma=False
    )
```

profile of v0, /device:TPU:0, one launch (start us, length us, event | category | flops | bytes accessed | tf_op | source)
XLA Modules:
  0.0 314.7 jit_solution(16939532329908146494)
XLA Ops:
  6.5 0.7 all-gather.4.cloned.1.call-update
  7.3 3.4 %copy.42 = bf16[2048,4,128]{2,0,1:T(8,128)(2,1)} copy(bf16[2048,4,128]{2,1,0:T(4,128)(2,1)} %param.11) | data formatting | bytes 4194304 | tf_op jit(solution)/shard_map/while | solution.py:51
  10.7 1.6 copy.43
  12.6 39.4 %all-gather.4.cloned.1.call-done = bf16[192,32,128]{2,1,0:T(8,128)(2,1)} async-done(((bf16[12,32,128]{2,1,0:T(8,128)(2,1)}), bf16[192,32,128]{2,1,0:T(8,128)(2,1)}) %all-gather.4.cloned.1.call-update) | async-done | bytes 1572880 | tf_op jit(solution)/shard_map/all_gather | solution.py:33
  52.0 76.9 %while.14 = (s32[]{:T(128)}, f32[3,64,32,128]{3,2,1,0:T(8,128)}, f32[3,64,32]{1,2,0:T(8,128)S(1)}, f32[3,64,32]{1,2,0:T(8,128)S(1)}, bf16[3,64,32,128]{3,2,1,0:T...) while((s32[]{:T(128)}, f32[3,64,32,128]{3,2,1,0:T(8,128)}, ...), condition=%wide.region_3.4_spmd, body=%wide.region_0.3_spmd.sunk | while | flops 2181033984 | bytes 125437048 | solution.py:51
  52.0 4.2 %bitcast_reduce_fusion.4 = (f32[64,4,8]{2,0,1:T(8,128)S(1)}, f32[4,64,8,2048]{3,2,1,0:T(8,128)S(1)}) fusion(bf16[2048,4,128]{2,0,1:T(8,128)(2,1)} %get-tuple-element.171, bf16[3,64,32,128]{3,2,1,0:T(8,128)(2,1)} %get-tuple-element.170, s32[]{:T(128)} %get-tuple-element.158), kind=kOutput, calls=%fused_computation.8.clone.1 | convolution fusion | flops 1082128384 | bytes 19407360 | tf_op jit(solution)/shard_map/while/body/eval_jaxpr/bkgd,pkd->bkgp/dot_general | solution.py:40
  56.3 5.7 %copy-done.1 = f32[4,64,8,2048]{3,2,1,0:T(8,128)} copy-done((f32[4,64,8,2048]{3,2,1,0:T(8,128)}, f32[4,64,8,2048]{3,2,1,0:T(8,128)S(1)}, u32[]{:S(2)}) %copy-start.1) | copy-done | bytes 16777240 | tf_op jit(solution)/shard_map/while
  62.0 3.3 %fusion.45 = f32[64,4,8]{2,0,1:T(8,128)S(1)} fusion(f32[4,64,8,2048]{3,2,1,0:T(8,128)S(1)} %get-tuple-element.146, f32[64,4,8]{2,0,1:T(8,128)S(1)} %get-tuple-element.147), kind=kLoop, calls=%fused_computation.10.clone.1 | loop fusion | flops 12580864 | bytes 16793600 | tf_op jit(solution)/shard_map/while/body/eval_jaxpr/reduce_sum | solution.py:12
  65.4 9.9 %fusion.44 = f32[64,4,8,128]{3,2,0,1:T(8,128)} fusion(bf16[2048,4,128]{2,0,1:T(8,128)(2,1)} %get-tuple-element.172, f32[4,64,8,2048]{3,2,1,0:T(8,128)} %copy-done.1, f32[64,4,8]{2,0,1:T(8,128)S(1)} %get-tuple-element.147), kind=kOutput, calls=%fused_computation.18.clone.1 | convolution fusion | flops 1086324736 | bytes 19931136 | tf_op jit(solution)/shard_map/while/body/eval_jaxpr/bkgp,pkd->bkgd/dot_general | solution.py:13
  75.3 2.4 bitcast_dynamic-update-slice_fusion.5
  77.7 4.2 %bitcast_reduce_fusion.4 = (f32[64,4,8]{2,0,1:T(8,128)S(1)}, f32[4,64,8,2048]{3,2,1,0:T(8,128)S(1)}) fusion(bf16[2048,4,128]{2,0,1:T(8,128)(2,1)} %get-tuple-element.171, bf16[3,64,32,128]{3,2,1,0:T(8,128)(2,1)} %get-tuple-element.170, s32[]{:T(128)} %get-tuple-element.158), kind=kOutput, calls=%fused_computation.8.clone.1 | convolution fusion | flops 1082128384 | bytes 19407360 | tf_op jit(solution)/shard_map/while/body/eval_jaxpr/bkgd,pkd->bkgp/dot_general | solution.py:40
  81.9 5.7 %copy-done.1 = f32[4,64,8,2048]{3,2,1,0:T(8,128)} copy-done((f32[4,64,8,2048]{3,2,1,0:T(8,128)}, f32[4,64,8,2048]{3,2,1,0:T(8,128)S(1)}, u32[]{:S(2)}) %copy-start.1) | copy-done | bytes 16777240 | tf_op jit(solution)/shard_map/while
  87.6 3.3 %fusion.45 = f32[64,4,8]{2,0,1:T(8,128)S(1)} fusion(f32[4,64,8,2048]{3,2,1,0:T(8,128)S(1)} %get-tuple-element.146, f32[64,4,8]{2,0,1:T(8,128)S(1)} %get-tuple-element.147), kind=kLoop, calls=%fused_computation.10.clone.1 | loop fusion | flops 12580864 | bytes 16793600 | tf_op jit(solution)/shard_map/while/body/eval_jaxpr/reduce_sum | solution.py:12
  91.1 9.9 %fusion.44 = f32[64,4,8,128]{3,2,0,1:T(8,128)} fusion(bf16[2048,4,128]{2,0,1:T(8,128)(2,1)} %get-tuple-element.172, f32[4,64,8,2048]{3,2,1,0:T(8,128)} %copy-done.1, f32[64,4,8]{2,0,1:T(8,128)S(1)} %get-tuple-element.147), kind=kOutput, calls=%fused_computation.18.clone.1 | convolution fusion | flops 1086324736 | bytes 19931136 | tf_op jit(solution)/shard_map/while/body/eval_jaxpr/bkgp,pkd->bkgd/dot_general | solution.py:13
  101.0 2.4 bitcast_dynamic-update-slice_fusion.5
  103.4 4.2 %bitcast_reduce_fusion.4 = (f32[64,4,8]{2,0,1:T(8,128)S(1)}, f32[4,64,8,2048]{3,2,1,0:T(8,128)S(1)}) fusion(bf16[2048,4,128]{2,0,1:T(8,128)(2,1)} %get-tuple-element.171, bf16[3,64,32,128]{3,2,1,0:T(8,128)(2,1)} %get-tuple-element.170, s32[]{:T(128)} %get-tuple-element.158), kind=kOutput, calls=%fused_computation.8.clone.1 | convolution fusion | flops 1082128384 | bytes 19407360 | tf_op jit(solution)/shard_map/while/body/eval_jaxpr/bkgd,pkd->bkgp/dot_general | solution.py:40
  107.6 5.7 %copy-done.1 = f32[4,64,8,2048]{3,2,1,0:T(8,128)} copy-done((f32[4,64,8,2048]{3,2,1,0:T(8,128)}, f32[4,64,8,2048]{3,2,1,0:T(8,128)S(1)}, u32[]{:S(2)}) %copy-start.1) | copy-done | bytes 16777240 | tf_op jit(solution)/shard_map/while
  113.3 3.3 %fusion.45 = f32[64,4,8]{2,0,1:T(8,128)S(1)} fusion(f32[4,64,8,2048]{3,2,1,0:T(8,128)S(1)} %get-tuple-element.146, f32[64,4,8]{2,0,1:T(8,128)S(1)} %get-tuple-element.147), kind=kLoop, calls=%fused_computation.10.clone.1 | loop fusion | flops 12580864 | bytes 16793600 | tf_op jit(solution)/shard_map/while/body/eval_jaxpr/reduce_sum | solution.py:12
  116.7 9.9 %fusion.44 = f32[64,4,8,128]{3,2,0,1:T(8,128)} fusion(bf16[2048,4,128]{2,0,1:T(8,128)(2,1)} %get-tuple-element.172, f32[4,64,8,2048]{3,2,1,0:T(8,128)} %copy-done.1, f32[64,4,8]{2,0,1:T(8,128)S(1)} %get-tuple-element.147), kind=kOutput, calls=%fused_computation.18.clone.1 | convolution fusion | flops 1086324736 | bytes 19931136 | tf_op jit(solution)/shard_map/while/body/eval_jaxpr/bkgp,pkd->bkgd/dot_general | solution.py:13
  126.6 2.3 bitcast_dynamic-update-slice_fusion.5
  129.1 0.6 gather_fusion.1
  129.7 2.0 gather_fusion.2
  131.6 9.1 %fusion.32 = (f32[12,4,8]{2,1,0:T(4,128)S(1)}, f32[12,4,8,1024]{3,2,1,0:T(8,128)}) fusion(bf16[12,4,1024,128]{3,2,1,0:T(8,128)(2,1)} %param.13, bf16[12,32,128]{2,1,0:T(8,128)(2,1)S(1)} %gather_fusion.2, pred[12,1024]{1,0:T(8,128)(4,1)S(1)} %iota_compare_fusion), kind=kOutput, calls=%fused_computation.53 | convolution fusion | flops 101842560 | bytes 14267904 | tf_op jit(solution)/shard_map/bkgd,bksd->bkgs/dot_general | solution.py:60
  140.9 1.8 fusion.17
  143.0 0.8 scatter_custom_fusion.2
  144.2 0.8 reduce.10
  145.0 0.7 reshape.221
  145.7 3.6 %all-to-all-start.2 = ((f32[16,1,384]{2,1,0:T(1,128)}), f32[16,1,384]{2,1,0:T(1,128)S(1)}, u32[]{:S(2)}, u32[]{:S(2)}) async-start(f32[16,1,384]{2,1,0:T(1,128)} %reshape.221), calls=%async_computation.2 | async-start | bytes 49152 | tf_op jit(solution)/shard_map/all_to_all | solution.py:82
  149.3 0.7 scatter_custom_fusion.1
  150.1 0.8 reduce.12
  150.9 0.7 reshape.219
  151.6 2.4 gather_fusion
  154.0 1.9 all-to-all-done.2
  155.9 4.1 %all-to-all-start.1 = ((f32[16,1,384]{2,1,0:T(1,128)}), f32[16,1,384]{2,1,0:T(1,128)S(1)}, u32[]{:S(2)}, u32[]{:S(2)}) async-start(f32[16,1,384]{2,1,0:T(1,128)} %reshape.219), calls=%async_computation.1 | async-start | bytes 49152 | tf_op jit(solution)/shard_map/all_to_all | solution.py:81
  160.1 6.9 %fusion.20 = f32[12,32,128]{2,1,0:T(8,128)S(1)} fusion(bf16[12,4,1024,128]{3,2,1,0:T(8,128)(2,1)} %param.14, f32[12,4,8,1024]{3,2,1,0:T(8,128)} %get-tuple-element.98, f32[12,4,8]{2,1,0:T(4,128)S(1)} %get-tuple-element.97, f32[12,32,128]{2,1,0:T(8,128)S(1)} %gather_fusion, f32[12,32]{1,0:T(8,128)S(1)} %get-tuple-element.96, f32[12,32]{1,0:T(8,128)S(1)} %get-tuple-element.95), kind=kOutput, calls=%fused_computation.32 | convolution fusion | flops 101597184 | bytes 14553600 | tf_op jit(solution)/shard_map/bkgs,bksd->bkgd/dot_general | solution.py:13
  167.0 2.3 scatter_fusion
  169.3 6.0 %all-to-all-start = ((f32[1,192,32,128]{3,2,0,1:T(8,128)}), f32[1,192,32,128]{3,2,0,1:T(8,128)}, u32[]{:S(2)}, u32[]{:S(2)}) async-start(f32[1,192,32,128]{3,2,0,1:T(8,128)} %bitcast.103), calls=%async_computation | async-start | bytes 6291456 | tf_op jit(solution)/shard_map/all_to_all | solution.py:80
  175.4 0.6 reduce.11
  176.7 0.9 bitcast_reduce_fusion.1
  177.6 0.6 reduce.13
  178.4 0.9 bitcast_reduce_fusion.2
  179.4 55.4 %all-to-all-done = f32[1,192,32,128]{3,2,0,1:T(8,128)} async-done(((f32[1,192,32,128]{3,2,0,1:T(8,128)}), f32[1,192,32,128]{3,2,0,1:T(8,128)}, u32[]{:S(2)}, u32[]{:S(2)}) %all-to-all-start) | async-done | bytes 3145760 | tf_op jit(solution)/shard_map/all_to_all | solution.py:80
  234.8 2.4 multiply_reduce_fusion
  237.3 0.7 reshape.186
  238.1 52.2 %all-gather.6.cloned.1.call-done = bf16[16,12,4096]{2,1,0:T(8,128)(2,1)} async-done(((bf16[1,12,4096]{2,1,0:T(8,128)(2,1)}), bf16[16,12,4096]{2,1,0:T(8,128)(2,1)}) %all-gather.6.cloned.1.call-update) | async-done | bytes 1572880 | tf_op jit(solution)/shard_map/all_gather | solution.py:91
  290.3 3.6 %reshape.187 = bf16[192,4096]{1,0:T(8,128)(2,1)} reshape(bf16[16,12,4096]{2,1,0:T(8,128)(2,1)} %all-gather.6.cloned.1.call-done) | data formatting | bytes 3145728
  293.9 3.3 %fusion.33 = f32[192,320]{1,0:T(8,128)} fusion(bf16[192,4096]{1,0:T(8,128)(2,1)} %reshape.187, bf16[4096,320]{0,1:T(8,128)(2,1)S(1)} %copy-done), kind=kOutput, calls=%fused_computation.56 | convolution fusion | flops 503316480 | bytes 4440064 | tf_op jit(solution)/shard_map/dot_general | solution.py:90
  297.2 11.0 %reduce-scatter.2.cloned.1.call-done = f32[96,320]{1,0:T(8,128)} async-done(((f32[192,320]{1,0:T(8,128)}), f32[96,320]{1,0:T(8,128)}) %reduce-scatter.2.cloned.1.call-update) | async-done | bytes 122896 | tf_op jit(solution)/shard_map/reduce_scatter | solution.py:95
  (50 shorter events, 3.1 us)
Async XLA Ops:
  6.5 287.4 %copy-start = (bf16[4096,320]{0,1:T(8,128)(2,1)S(1)}, bf16[4096,320]{0,1:T(8,128)(2,1)}, u32[]{:S(2)}) copy-start(bf16[4096,320]{0,1:T(8,128)(2,1)} %param.17) | copy-start | bytes 7864324
  6.5 45.5 %all-gather.4.cloned.1.call-start = ((), (), s32[]{:S(2)}) async-start(), calls=%async_computation.4 | async-start | bytes 1671168 | tf_op jit(solution)/shard_map/all_gather | solution.py:33
  7.3 3.4 %copy-start.2 = (bf16[2048,4,128]{2,1,0:T(4,128)(2,1)S(1)}, bf16[2048,4,128]{2,1,0:T(4,128)(2,1)}, u32[]{:S(2)}) copy-start(bf16[2048,4,128]{2,1,0:T(4,128)(2,1)} %param.12) | copy-start | bytes 6291460
  10.7 1.6 copy-start.3
  10.7 1.8 copy-start.4
  56.2 5.7 %copy-start.1 = (f32[4,64,8,2048]{3,2,1,0:T(8,128)}, f32[4,64,8,2048]{3,2,1,0:T(8,128)S(1)}, u32[]{:S(2)}) copy-start(f32[4,64,8,2048]{3,2,1,0:T(8,128)S(1)} %get-tuple-element.146) | copy-start | bytes 50331652 | tf_op jit(solution)/shard_map/while
  81.9 5.7 %copy-start.1 = (f32[4,64,8,2048]{3,2,1,0:T(8,128)}, f32[4,64,8,2048]{3,2,1,0:T(8,128)S(1)}, u32[]{:S(2)}) copy-start(f32[4,64,8,2048]{3,2,1,0:T(8,128)S(1)} %get-tuple-element.146) | copy-start | bytes 50331652 | tf_op jit(solution)/shard_map/while
  107.6 5.7 %copy-start.1 = (f32[4,64,8,2048]{3,2,1,0:T(8,128)}, f32[4,64,8,2048]{3,2,1,0:T(8,128)S(1)}, u32[]{:S(2)}) copy-start(f32[4,64,8,2048]{3,2,1,0:T(8,128)S(1)} %get-tuple-element.146) | copy-start | bytes 50331652 | tf_op jit(solution)/shard_map/while
  145.7 10.2 %all-to-all-start.2 = ((f32[16,1,384]{2,1,0:T(1,128)}), f32[16,1,384]{2,1,0:T(1,128)S(1)}, u32[]{:S(2)}, u32[]{:S(2)}) async-start(f32[16,1,384]{2,1,0:T(1,128)} %reshape.221), calls=%async_computation.2 | async-start | bytes 49152 | tf_op jit(solution)/shard_map/all_to_all | solution.py:82
  155.9 13.4 %all-to-all-start.1 = ((f32[16,1,384]{2,1,0:T(1,128)}), f32[16,1,384]{2,1,0:T(1,128)S(1)}, u32[]{:S(2)}, u32[]{:S(2)}) async-start(f32[16,1,384]{2,1,0:T(1,128)} %reshape.219), calls=%async_computation.1 | async-start | bytes 49152 | tf_op jit(solution)/shard_map/all_to_all | solution.py:81
  169.3 65.5 %all-to-all-start = ((f32[1,192,32,128]{3,2,0,1:T(8,128)}), f32[1,192,32,128]{3,2,0,1:T(8,128)}, u32[]{:S(2)}, u32[]{:S(2)}) async-start(f32[1,192,32,128]{3,2,0,1:T(8,128)} %bitcast.103), calls=%async_computation | async-start | bytes 6291456 | tf_op jit(solution)/shard_map/all_to_all | solution.py:80
  175.3 115.0 %all-gather.6.cloned.1.call-start = ((), (), s32[]{:S(2)}) async-start(), calls=%async_computation.6 | async-start | bytes 2228224 | tf_op jit(solution)/shard_map/all_gather | solution.py:91
  238.1 70.1 %reduce-scatter.2.cloned.1.call-start = ((), (), s32[]{:S(2)}) async-start(), calls=%async_computation.5 | async-start | bytes 442368 | tf_op jit(solution)/shard_map/reduce_scatter | solution.py:95
Sparse Core Ops, SparseCore 0:
  9.6 42.3 all-gather.3
  238.2 52.1 all-gather.5
  297.3 10.7 reduce-scatter.1
where the time goes:
time: 316 us; the launch traced here: 315 us
  waiting for transfers between devices  161 us (51%)
  matrix products  61.6 us (19%)
  local copies, waits for them, and re-layouts  46.5 us (15%)
  other arithmetic  18.8 us (6%)
  starting transfers between devices  13.9 us (4%)
  between operations  13.4 us (4%)
    all_to_all x1, waiting for transfers between devices, per_device(): lax.all_to_all(pre_out[None], 'seq', split_axis=1, concat_axis=0, tiled=T...  55.4 us
    all_gather x1, waiting for transfers between devices, per_device(): lax.all_gather(attention, 'seq', axis=0, tiled=True)  52.2 us
    all_gather x1, waiting for transfers between devices, per_device(): all_queries = lax.all_gather(queries, 'seq', axis=0, tiled=True)  39.4 us
    dot_general x4, matrix products, partial_softmax(): jnp.einsum(equation, weights.astype(jnp.bfloat16), values_block, preferre...  36.6 us
    while x6, local copies, waits for them, and re-layouts  17.1 us
    dot_general x3, matrix products, prefix_block(): jnp.einsum('bkgd,pkd->bkgp', grouped, prompt_keys, preferred_element_type...  12.6 us
    reduce_sum x4, other arithmetic, partial_softmax(): row_total = jnp.sum(weights, axis=-1)  11.7 us
    reduce_scatter x1, waiting for transfers between devices, per_device(): return lax.psum_scatter(terms, 'head', scatter_dimension=0, tiled=True)  11 us
  transfers between devices with their start and end apart: 6, of which 5 were waited for; matrix products, arithmetic and copies ran while one was open for 7% of the time, Pallas kernels for 0%

commit v1 on v0

--- a/solution.py
+++ b/solution.py
@@ -1,9 +1,495 @@
+import functools
 import math
 
 import jax
 import jax.numpy as jnp
 from jax import lax
+from jax.experimental import pallas as pl
+from jax.experimental.pallas import tpu as pltpu
 from jax.sharding import PartitionSpec as P
+
+MESH = pl.DeviceIdType.MESH
+NT = (((1,), (1,)), ((), ()))
+TN = (((0,), (0,)), ((), ()))
+NN = (((1,), (0,)), ((), ()))
+LOW = -1e30
+ZS, YS, CS = 4, 2, 2
+
+
+def dot(a, b, dims):
+    return lax.dot_general(a, b, dims, preferred_element_type=jnp.float32)
+
+
+def merge(parts, unit):
+    top = functools.reduce(jnp.maximum, [part[1] for part in parts])
+    out, total = None, None
+    for part_out, part_top, part_total in parts:
+        factor = jnp.exp2((part_top - top) * unit)
+        scaled, count = part_out * factor, part_total * factor
+        out = scaled if out is None else out + scaled
+        total = count if total is None else total + count
+    return out, top, total
+
+
+def kernel(
+    unit,
+    q_in,
+    keys_in,
+    values_in,
+    tail_keys_in,
+    tail_values_in,
+    lengths,
+    column_key,
+    perm,
+    weight_in,
+    out,
+    q_all,
+    keys,
+    values,
+    tail_keys,
+    tail_values,
+    weight,
+    own_q,
+    tail_rows,
+    tail_m,
+    tail_l,
+    tail_out,
+    tail_stat,
+    part,
+    stat,
+    core_part,
+    core_stat,
+    y_own,
+    y_send,
+    y_part,
+    y_own_stat,
+    y_send_stat,
+    y_stat,
+    z_send,
+    z_send_stat,
+    z_part,
+    z_stat,
+    att,
+    total,
+    x_part,
+    load_sem,
+    tail_sem,
+    q_sems,
+    qz_send_sem,
+    qz_recv_sem,
+    core_sems,
+    y_sems,
+    zs_send,
+    zs_recv,
+    zo_sems,
+    az_send,
+    az_recv,
+    a_sems,
+    x_sems,
+):
+    kv_count, rows_local, width = q_in.shape
+    slots = lengths.shape[0]
+    group = rows_local // slots
+    chunk = YS * CS * rows_local
+    tail_len = tail_keys.shape[2]
+    seq, head = lax.axis_index("seq"), lax.axis_index("head")
+    z, y, core = seq // (YS * CS), (seq // CS) % YS, seq % CS
+    other_y, other_core, other_head = 1 - y, 1 - core, 1 - head
+
+    def at(z_to, y_to, core_to):
+        return ((z_to * YS + y_to) * CS + core_to, head)
+
+    z_peers = [at((z + step) % ZS, y, core) for step in range(1, ZS)]
+    y_peer, core_peer, x_peer = at(z, other_y, core), at(z, y, other_core), (seq, other_head)
+    order = [(3 * turn) % kv_count for turn in range(kv_count)]
+
+    def remote(source, target, send, recv, device):
+        return pltpu.make_async_remote_copy(
+            src_ref=source, dst_ref=target, send_sem=send, recv_sem=recv, device_id=device, device_id_type=MESH
+        )
+
+    loads = [
+        pltpu.make_async_copy(keys_in, keys, load_sem.at[0]),
+        pltpu.make_async_copy(values_in, values, load_sem.at[1]),
+        pltpu.make_async_copy(weight_in, weight, load_sem.at[2]),
+    ]
+
+    def tail_loads(k):
+        return [
+            pltpu.make_async_copy(tail_keys_in.at[:, k], tail_keys.at[k], tail_sem.at[k, 0]),
+            pltpu.make_async_copy(tail_values_in.at[:, k], tail_values.at[k], tail_sem.at[k, 1]),
+        ]
+
+    loads[0].start()
+    loads[1].start()
+    for k in order:
+        for load in tail_loads(k):
+            load.start()
+    loads[2].start()
+
+    barrier = pltpu.get_barrier_semaphore()
+    peers = z_peers + [y_peer, core_peer, x_peer]
+    for peer in peers:
+        pl.semaphore_signal(barrier, inc=1, device_id=peer, device_id_type=MESH)
+    pl.semaphore_wait(barrier, len(peers))
+
+    def q_z(k):
+        return [
+            remote(q_in.at[k], q_all.at[k, z, y, core], qz_send_sem.at[k, i], qz_recv_sem.at[k, i], z_peers[i])
+            for i in range(ZS - 1)
+        ]
+
+    def q_y(k):
+        mine = q_all.at[k, :, y, core]
+        return remote(mine, mine, q_sems.at[k, 0], q_sems.at[k, 1], y_peer)
+
+    def q_core(k):
+        mine = q_all.at[k, :, :, core]
+        return remote(mine, mine, q_sems.at[k, 2], q_sems.at[k, 3], core_peer)
+
+    for k in order:
+        for copy in q_z(k):
+            copy.start()
+    for k in order:
+        q_all[k, z, y, core] = q_in[k]
+
+    def q_after_z(k):
+        for copy in q_z(k):
+            copy.wait()
+        q_y(k).start()
+
+    def q_after_y(k):
+        q_y(k).wait()
+        q_core(k).start()
+
+    def q_ready(k):
+        q_core(k).wait()
+
+    def tail(k):
+        for load in tail_loads(k):
+            load.wait()
+        columns = column_key.shape[1]
+        row_key = seq * rows_local + lax.broadcasted_iota(jnp.int32, (rows_local, columns), 0)
+        match = column_key[...] == row_key
+        pick = jnp.where(match, 1.0, 0.0).astype(jnp.bfloat16)
+        every = q_all[k].reshape(columns, width)
+        own_q[...] = dot(pick, every, NN)
+
+        def one(t, carry):
+            rows = pl.ds(pl.multiple_of(t * group, group), group)
+            scores = dot(own_q[rows, :].astype(jnp.bfloat16), tail_keys[k, t], NT)
+            position = lax.broadcasted_iota(jnp.int32, scores.shape, 1)
+            scores = jnp.where(position < lengths[t], scores, LOW)
+            top = jnp.max(scores, axis=1, keepdims=True)
+            weights = jnp.exp2((scores - top) * unit)
+            tail_rows[rows, :] = dot(weights.astype(jnp.bfloat16), tail_values[k, t], NN)
+            tail_m[rows, :] = jnp.broadcast_to(top, (group, width))
+            tail_l[rows, :] = jnp.broadcast_to(jnp.sum(weights, axis=1, keepdims=True), (group, width))
+            return carry
+
+        lax.fori_loop(0, slots, one, 0, unroll=4)
+        for c in range(columns // chunk):
+            span = slice(c * chunk, (c + 1) * chunk)
+            here = column_key[:, span] == row_key[:, span]
+            tail_out[c] = dot(tail_rows[...].astype(jnp.bfloat16), jnp.where(here, 1.0, 0.0).astype(jnp.bfloat16), TN)
+            top = jnp.max(jnp.where(here, tail_m[:, :1], LOW), axis=0, keepdims=True)
+            count = jnp.sum(jnp.where(here, tail_l[:, :1], 0.0), axis=0, keepdims=True)
+            tail_stat[c, 0:1] = top
+            tail_stat[c, 1:2] = count
+
+    def prompt(k, pair):
+        q = q_all[k, pl.ds(pair * 2, 2)].reshape(2 * chunk, width)
+        scores = dot(keys[k], q, NT)
+        top = jnp.max(scores, axis=0, keepdims=True)
+        weights = jnp.exp2((scores - top) * unit)
+        count = jnp.sum(weights, axis=0, keepdims=True)
+        rows = dot(values[k], weights.astype(jnp.bfloat16), NN)
+        for c in range(2):
+            span = slice(c * chunk, (c + 1) * chunk)
+            at_chunk = pair * 2 + c
+            o, m, l = merge(
+                [
+                    (rows[:, span], top[:, span], count[:, span]),
+                    (tail_out[at_chunk], tail_stat[at_chunk, 0:1], tail_stat[at_chunk, 1:2]),
+                ],
+                unit,
+            )
+            part[k, pair, c] = o.astype(jnp.bfloat16)
+            stat[k, pair, c, 0:1] = m
+            stat[k, pair, c, 1:2] = l
+
+    def sum_core(k):
+        return [
+            remote(part.at[k, :, other_core], core_part.at[k], core_sems.at[k, 0], core_sems.at[k, 1], core_peer),
+            remote(stat.at[k, :, other_core], core_stat.at[k], core_sems.at[k, 2], core_sems.at[k, 3], core_peer),
+        ]
+
+    def sum_y(k):
+        return [
+            remote(y_send.at[k], y_part.at[k], y_sems.at[k, 0], y_sems.at[k, 1], y_peer),
+            remote(y_send_stat.at[k], y_stat.at[k], y_sems.at[k, 2], y_sems.at[k, 3], y_peer),
+        ]
+
+    def sum_z(k):
+        slot = (z - k + ZS - 1) % ZS
+        return [
+            remote(z_send.at[k], z_part.at[slot], zs_send.at[k, 0], zs_recv.at[slot, 0], at(k, y, core)),
+            remote(z_send_stat.at[k], z_stat.at[slot], zs_send.at[k, 1], zs_recv.at[slot, 1], at(k, y, core)),
+        ]
+
+    def att_z(k):
+        mine = att.at[k, y, core]
+        return [
+            remote(mine, mine, az_send.at[i], az_recv.at[k], at((k + 1 + i) % ZS, y, core)) for i in range(ZS - 1)
+        ]
+
+    def att_y(k):
+        mine = att.at[k, y, core]
+        return remote(mine, mine, a_sems.at[k, 0], a_sems.at[k, 1], y_peer)
+
+    def att_core(k):
+        mine = att.at[k, :, core]
+        return remote(mine, mine, a_sems.at[k, 2], a_sems.at[k, 3], core_peer)
+
+    def step_a(k):
+        for copy in sum_core(k):
+            copy.start()
+
+    def step_b(k):
+        for copy in sum_core(k):
+            copy.wait()
+
+        def joined(i):
+            return merge(
+                [
+                    (part[k, i, core].astype(jnp.float32), stat[k, i, core, 0:1], stat[k, i, core, 1:2]),
+                    (core_part[k, i].astype(jnp.float32), core_stat[k, i, 0:1], core_stat[k, i, 1:2]),
+                ],
+                unit,
+            )
+
+        o, m, l = joined(other_y)
+        y_send[k] = o.astype(jnp.bfloat16)
+        y_send_stat[k, 0:1] = m
+        y_send_stat[k, 1:2] = l
+        for copy in sum_y(k):
+            copy.start()
+        o, m, l = joined(y)
+        y_own[k] = o
+        y_own_stat[k, 0:1] = m
+        y_own_stat[k, 1:2] = l
+
+    def step_c(k):
+        for copy in sum_y(k):
+            copy.wait()
+        o, m, l = merge(
+            [
+                (y_own[k], y_own_stat[k, 0:1], y_own_stat[k, 1:2]),
+                (y_part[k].astype(jnp.float32), y_stat[k, 0:1], y_stat[k, 1:2]),
+            ],
+            unit,
+        )
+        y_own[k] = o
+        z_send[k] = o.astype(jnp.bfloat16)
+        z_send_stat[k, 0:1] = m
+        z_send_stat[k, 1:2] = l
+
+        @pl.when(z != k)
+        def _():
+            for copy in sum_z(k):
+                copy.start()
+
+    def step_d(k):
+        @pl.when(z != k)
+        def _():
+            for copy in sum_z(k):
+                copy.wait_send()
+
+        @pl.when(z == k)
+        def _():
+            parts = [(y_own[k], z_send_stat[k, 0:1], z_send_stat[k, 1:2])]
+            for slot in range(ZS - 1):
+                device = at(k, y, core)
+                remote(z_send.at[k], z_part.at[slot], zs_send.at[k, 0], zs_recv.at[slot, 0], device).wait_recv()
+                remote(z_send_stat.at[k], z_stat.at[slot], zs_send.at[k, 1], zs_recv.at[slot, 1], device).wait_recv()
+                parts.append((z_part[slot].astype(jnp.float32), z_stat[slot, 0:1], z_stat[slot, 1:2]))
+            o, _, l = merge(parts, unit)
+            attention = (o / l).astype(jnp.bfloat16)
+            rows = dot(perm[...], attention, NT).astype(jnp.bfloat16)
+            att[k, y, core] = rows.reshape(att.shape[3:])
+            for copy in att_z(k):
+                copy.start()
+
+    def step_e(k):
+        @pl.when(z != k)
+        def _():
+            att_z(k)[0].wait_recv()
+
+        att_y(k).start()
+
+    def step_f(k):
+        @pl.when(z == k)
+        def _():
+            for copy in att_z(k):
+                copy.wait_send()
+
+        att_y(k).wait()
+        att_core(k).start()
+
+    def step_g(k):
+        att_core(k).wait()
+        value = None
+        for g in range(0, group, 2):
+            block = jnp.concatenate(
+                [
+                    jnp.concatenate([att[k, i, j, g + h] for i in range(YS) for j in range(CS)], axis=0)
+                    for h in range(2)
+                ],
+                axis=1,
+            )
+            first = (k * group + g) * width
+            term = dot(block, weight[first : first + 2 * width, :], NN)
+            value = term if value is None else value + term
+        return value
+
+    a, b, c, d = order
+    q_after_z(a)
+    q_after_z(b)
+    q_after_y(a)
+    loads[0].wait()
+    loads[1].wait()
+    q_ready(a)
+
+    hooks = {
+        0: [(q_after_z, c), (q_after_y, b)],
+        1: [(step_a, a), (q_after_z, d), (q_after_y, c), (q_ready, b)],
+        2: [(step_b, a), (q_after_y, d)],
+        3: [(step_c, a), (step_a, b), (q_ready, c)],
+        4: [(step_d, a), (step_b, b)],
+        5: [(step_e, a), (step_c, b), (step_a, c), (q_ready, d)],
+        6: [(step_f, a), (step_d, b), (step_b, c)],
+        7: [(step_a, d), (step_e, b), (step_c, c)],
+    }
+
+    def turn(i, carry):
+        k, pair = (3 * (i // 2)) % kv_count, i % 2
+
+        @pl.when(pair == 0)
+        def _():
+            tail(k)
+
+        prompt(k, pair)
+        for at_turn, calls in hooks.items():
+
+            @pl.when(i == at_turn)
+            def _(calls=calls):
+                for call, at_k in calls:
+                    call(at_k)
+
+        return carry
+
+    lax.fori_loop(0, 2 * kv_count, turn, 0)
+    step_b(d)
+    step_d(c)
+    step_f(b)
+    step_c(d)
+    loads[2].wait()
+    value = step_g(a)
+    step_e(c)
+    step_d(d)
+    value += step_g(b)
+    step_f(c)
+    step_e(d)
+    value += step_g(c)
+    step_f(d)
+    value += step_g(d)
+    half = value.shape[0] // 2
+    total[0] = value[:half]
+    total[1] = value[half:]
+    swap = remote(total.at[other_head], x_part, x_sems.at[0], x_sems.at[1], x_peer)
+    swap.start()
+    swap.wait()
+    out[...] = total[head] + x_part[...]
+
+
+def fused(queries, prompt_keys, prompt_values, suffix_keys, suffix_values, suffix_lengths, slot_of_sample, out_weight):
+    slots, heads, width = queries.shape
+    kv = prompt_keys.shape[1]
+    group = heads // kv
+    rows = slots * group
+    positions = prompt_keys.shape[0]
+    samples = slot_of_sample.shape[0]
+    columns = samples * group
+    chunk = YS * CS * rows
+    share = chunk // group
+    tail_len = suffix_keys.shape[2]
+    half, out_columns = samples // 2, out_weight.shape[1]
+    unit = math.log2(math.e) / math.sqrt(width)
+
+    q = queries.reshape(slots, kv, group, width).transpose(1, 0, 2, 3).reshape(kv, rows, width)
+    keys = prompt_keys.transpose(1, 0, 2)
+    values = prompt_values.transpose(1, 2, 0)
+    column_key = (slot_of_sample[:, None] * group + jnp.arange(group, dtype=jnp.int32)).reshape(1, columns)
+    place = jnp.arange(chunk, dtype=jnp.int32)
+    perm = (((place % share) * group + place // share)[:, None] == place[None, :]).astype(jnp.bfloat16)
+
+    bf16, f32 = jnp.bfloat16, jnp.float32
+    vmem, hbm = pl.BlockSpec(memory_space=pltpu.VMEM), pl.BlockSpec(memory_space=pl.ANY)
+    sem = pltpu.SemaphoreType.DMA
+    return pl.pallas_call(
+        functools.partial(kernel, unit),
+        out_shape=jax.ShapeDtypeStruct((half, out_columns), f32),
+        in_specs=[vmem, hbm, hbm, hbm, hbm, pl.BlockSpec(memory_space=pltpu.SMEM), vmem, vmem, hbm],
+        out_specs=vmem,
+        scratch_shapes=[
+            pltpu.VMEM((kv, ZS, YS, CS, rows, width), bf16),
+            pltpu.VMEM(keys.shape, bf16),
+            pltpu.VMEM(values.shape, bf16),
+            pltpu.VMEM((kv, slots, tail_len, width), bf16),
+            pltpu.VMEM((kv, slots, tail_len, width), bf16),
+            pltpu.VMEM(out_weight.shape, bf16),
+            pltpu.VMEM((rows, width), f32),
+            pltpu.VMEM((rows, width), f32),
+            pltpu.VMEM((rows, width), f32),
+            pltpu.VMEM((rows, width), f32),
+            pltpu.VMEM((ZS, width, chunk), f32),
+            pltpu.VMEM((ZS, 8, chunk), f32),
+            pltpu.VMEM((kv, YS, CS, width, chunk), bf16),
+            pltpu.VMEM((kv, YS, CS, 8, chunk), f32),
+            pltpu.VMEM((kv, YS, width, chunk), bf16),
+            pltpu.VMEM((kv, YS, 8, chunk), f32),
+            pltpu.VMEM((kv, width, chunk), f32),
+            pltpu.VMEM((kv, width, chunk), bf16),
+            pltpu.VMEM((kv, width, chunk), bf16),
+            pltpu.VMEM((kv, 8, chunk), f32),
+            pltpu.VMEM((kv, 8, chunk), f32),
+            pltpu.VMEM((kv, 8, chunk), f32),
+            pltpu.VMEM((kv, width, chunk), bf16),
+            pltpu.VMEM((kv, 8, chunk), f32),
+            pltpu.VMEM((ZS - 1, width, chunk), bf16),
+            pltpu.VMEM((ZS - 1, 8, chunk), f32),
+            pltpu.VMEM((kv, YS, CS, group, share, width), bf16),
+            pltpu.VMEM((2, half, out_columns), f32),
+            pltpu.VMEM((half, out_columns), f32),
+            sem((3,)),
+            sem((kv, 2)),
+            sem((kv, 4)),
+            sem((kv, ZS - 1)),
+            sem((kv, ZS - 1)),
+            sem((kv, 4)),
+            sem((kv, 4)),
+            sem((kv, 2)),
+            sem((ZS - 1, 2)),
+            sem((1,)),
+            sem((ZS - 1,)),
+            sem((kv,)),
+            sem((kv, 4)),
+            sem((2,)),
+        ],
+        compiler_params=pltpu.CompilerParams(
+            collective_id=0, has_side_effects=True, vmem_limit_bytes=62 * 1024 * 1024
+        ),
+    )(q, keys, values, suffix_keys, suffix_values, suffix_lengths, column_key, perm, out_weight)
 
 
 def partial_softmax(scores, values_block, equation):
@@ -106,6 +592,10 @@
         P(),
         P("head", "seq"),
     )
-    return jax.shard_map(
-        per_device, mesh=mesh, in_specs=placed, out_specs=P("head", "seq"), check_vma=False
-    )
+
+    def body(*arrays):
+        kv = arrays[1].shape[1]
+        fits = mesh.shape["seq"] == ZS * YS * CS and mesh.shape["head"] == 2 and kv == ZS
+        return (fused if fits else per_device)(*arrays)
+
+    return jax.shard_map(body, mesh=mesh, in_specs=placed, out_specs=P("head", "seq"), check_vma=False)

time: 316 us -> 114 us (0.36)
  waiting for transfers between devices: 161 us -> 0 us
  Pallas kernels: 0 us -> 98.5 us
  matrix products: 61.6 us -> 0 us
  local copies, waits for them, and re-layouts: 46.5 us -> 13.5 us
  other arithmetic: 18.8 us -> 1.64 us
  starting transfers between devices: 13.9 us -> 0 us
  between operations: 13.4 us -> 0.02 us
    pallas_call x0 -> x1, Pallas kernels: none -> 98.5 us  [fused(): pl.pallas_call(functools.partial(kernel, unit), out_shape=jax.ShapeDtypeS...]
    all_gather x2 -> x0, waiting for transfers between devices: 91.6 us -> none  [the longest x1 52.2 us: per_device(): lax.all_gather(attention, 'seq', axis=0, tiled=True)]
    dot_general x9 -> x0, matrix products: 61.6 us -> none  [the longest x4 36.6 us: partial_softmax(): jnp.einsum(equation, weights.astype(jnp.bfloat16), values_block, preferre...]
    all_to_all x3 -> x0, waiting for transfers between devices: 57.3 us -> none  [the longest x1 55.4 us: per_device(): lax.all_to_all(pre_out[None], 'seq', split_axis=1, concat_axis=0, tiled=T...]
    while x10 -> x0, local copies, waits for them, and re-layouts: 22.3 us -> none
    reduce_sum x7 -> x0, other arithmetic: 14.3 us -> none  [the longest x4 11.7 us: partial_softmax(): row_total = jnp.sum(weights, axis=-1)]
    all_to_all x3 -> x0, starting transfers between devices: 13.8 us -> none  [the longest x1 6.04 us: per_device(): lax.all_to_all(pre_out[None], 'seq', split_axis=1, concat_axis=0, tiled=T...]
    reduce_scatter x1 -> x0, waiting for transfers between devices: 11 us -> none  [per_device(): return lax.psum_scatter(terms, 'head', scatter_dimension=0, tiled=True)]
  transfers between devices with their start and end apart: 6 -> 0, of which waited for: 5 -> 0; matrix products, arithmetic and copies ran while one was open for 7% -> 0% of each run, Pallas kernels for 0% -> 0%
where the time goes in v1:
time: 114 us
  Pallas kernels  98.5 us (86%)
  local copies, waits for them, and re-layouts  13.5 us (12%)
  other arithmetic  1.64 us (1%)
    pallas_call x1, Pallas kernels, fused(): pl.pallas_call(functools.partial(kernel, unit), out_shape=jax.ShapeDtypeS...  98.5 us
    unnamed x8, local copies, waits for them, and re-layouts  12.1 us

profile of v1, /device:TPU:0, one launch (start us, length us, event | category | flops | bytes accessed | tf_op | source)
XLA Modules:
  0.0 113.6 jit_solution(7881322210691240606)
XLA Ops:
  0.0 0.0 copy-start
  0.0 0.7 broadcast_multiply_fusion
  0.7 0.1 iota_add_fusion
  0.8 0.7 add.48.column_key
  1.5 0.0 copy-done
  1.5 0.7 copy_bitcast_fusion.1.q_in
  2.2 0.8 fusion.perm
  3.0 3.2 %copy.19 = bf16[2048,4,128]{2,0,1:T(8,128)(2,1)} copy(bf16[2048,4,128]{2,1,0:T(4,128)(2,1)} %param.9) | data formatting | bytes 4194304 | tf_op args[1]
  6.2 0.0 copy-start.1
  6.2 4.5 %copy.15 = bf16[2048,4,128]{0,2,1:T(8,128)(2,1)} copy(bf16[2048,4,128]{2,1,0:T(4,128)(2,1)} %param.10) | data formatting | bytes 4194304 | tf_op args[2]
  10.8 0.0 copy-done.1
  10.8 2.8 %copy.16.weight_in = bf16[4096,320]{1,0:T(8,128)(2,1)} copy(bf16[4096,320]{0,1:T(8,128)(2,1)S(1)} %copy-done.1) | data formatting | bytes 5242880 | tf_op args[7]
  13.5 98.5 %shard_map.82 = f32[96,320]{1,0:T(8,128)} custom-call(bf16[4,96,128]{2,1,0:T(8,128)(2,1)} %copy_bitcast_fusion.1.q_in, bf16[4,2048,128]{2,1,0:T(8,128)(2,1)} %bitcast.11, bf16[4,128,2048]{2,1,0:T(8,128)(2,1)} %bitcast.12, bf16[12,4,1024,128]{3,2,1,0:T(8,128)(2,1)} %tail_keys_in.1, bf16[12,4,1024,128]{3,2,1,0:T(8,128)(2,1)} %tail_values_in.1, s32[12]{0:T(128)} %lengths.1, ...), custom_call_target="tpu_custom_call" | custom-call | tf_op jit(solution)/shard_map/pallas_call | solution.py:439
  112.0 1.6 %copy.21 = f32[96,320]{1,0:T(8,128)} copy(f32[96,320]{1,0:T(8,128)} %shard_map.82) | data formatting | bytes 245760
  (1 shorter events, 0.0 us)
Async XLA Ops:
  0.0 1.5 %copy-start = (bf16[12,32,128]{2,1,0:T(8,128)(2,1)S(1)}, bf16[12,32,128]{2,1,0:T(8,128)(2,1)}, u32[]{:S(2)}) copy-start(bf16[12,32,128]{2,1,0:T(8,128)(2,1)} %param.8) | copy-start | bytes 294916
  6.2 4.5 %copy-start.1 = (bf16[4096,320]{0,1:T(8,128)(2,1)S(1)}, bf16[4096,320]{0,1:T(8,128)(2,1)}, u32[]{:S(2)}) copy-start(bf16[4096,320]{0,1:T(8,128)(2,1)} %param.15) | copy-start | bytes 7864324

commit v2 on v1

--- a/solution.py
+++ b/solution.py
@@ -39,10 +39,14 @@
     tail_keys_in,
     tail_values_in,
     lengths,
-    column_key,
-    perm,
+    slot_of,
     weight_in,
     out,
+    q_own,
+    raw_keys,
+    raw_values,
+    perm,
+    match,
     q_all,
     keys,
     values,
@@ -50,9 +54,8 @@
     tail_values,
     weight,
     own_q,
+    tail_scores,
     tail_rows,
-    tail_m,
-    tail_l,
     tail_out,
     tail_stat,
     part,
@@ -87,11 +90,11 @@
     a_sems,
     x_sems,
 ):
-    kv_count, rows_local, width = q_in.shape
+    kv_count, rows_local, width = q_own.shape
     slots = lengths.shape[0]
     group = rows_local // slots
+    samples = slot_of.shape[1]
     chunk = YS * CS * rows_local
-    tail_len = tail_keys.shape[2]
     seq, head = lax.axis_index("seq"), lax.axis_index("head")
     z, y, core = seq // (YS * CS), (seq // CS) % YS, seq % CS
     other_y, other_core, other_head = 1 - y, 1 - core, 1 - head
@@ -109,8 +112,8 @@
         )
 
     loads = [
-        pltpu.make_async_copy(keys_in, keys, load_sem.at[0]),
-        pltpu.make_async_copy(values_in, values, load_sem.at[1]),
+        pltpu.make_async_copy(keys_in, raw_keys, load_sem.at[0]),
+        pltpu.make_async_copy(values_in, raw_values, load_sem.at[1]),
         pltpu.make_async_copy(weight_in, weight, load_sem.at[2]),
     ]
 
@@ -127,6 +130,18 @@
             load.start()
     loads[2].start()
 
+    def grid(shape, axis):
+        return lax.broadcasted_iota(jnp.int32, shape, axis)
+
+    def onehot(chosen):
+        return jnp.where(chosen, 1.0, 0.0).astype(jnp.bfloat16)
+
+    flat = q_in[...].reshape(-1, width)
+    shape = (rows_local, flat.shape[0])
+    place = (grid(shape, 0) // group) * (kv_count * group) + grid(shape, 0) % group
+    for k in order:
+        q_own[k] = dot(onehot(grid(shape, 1) == place + k * group), flat, NN).astype(jnp.bfloat16)
+
     barrier = pltpu.get_barrier_semaphore()
     peers = z_peers + [y_peer, core_peer, x_peer]
     for peer in peers:
@@ -135,7 +150,7 @@
 
     def q_z(k):
         return [
-            remote(q_in.at[k], q_all.at[k, z, y, core], qz_send_sem.at[k, i], qz_recv_sem.at[k, i], z_peers[i])
+            remote(q_own.at[k], q_all.at[k, z, y, core], qz_send_sem.at[k, i], qz_recv_sem.at[k, i], z_peers[i])
             for i in range(ZS - 1)
         ]
 
@@ -151,7 +166,7 @@
         for copy in q_z(k):
             copy.start()
     for k in order:
-        q_all[k, z, y, core] = q_in[k]
+        q_all[k, z, y, core] = q_own[k]
 
     def q_after_z(k):
         for copy in q_z(k):
@@ -165,45 +180,78 @@
     def q_ready(k):
         q_core(k).wait()
 
+    def split_keys():
+        size = 256 // kv_count
+        shape = (256, 256)
+        pick = onehot(grid(shape, 1) == (grid(shape, 0) % size) * kv_count + grid(shape, 0) // size)
+
+        def one(i, carry):
+            rows = raw_keys[pl.ds(pl.multiple_of(i * 256, 256), 256), :]
+            apart = dot(pick, rows, NN).astype(jnp.bfloat16)
+            for k in range(kv_count):
+                keys[k, pl.ds(pl.multiple_of(i * size, size), size), :] = apart[k * size : (k + 1) * size]
+            return carry
+
+        lax.fori_loop(0, raw_keys.shape[0] // 256, one, 0, unroll=4)
+
+    def split_values():
+        wide = 128 * kv_count
+        shape = (wide, wide)
+        pick = onehot(grid(shape, 0) == (grid(shape, 1) % 128) * kv_count + grid(shape, 1) // 128)
+
+        def one(i, carry):
+            rows = raw_values[pl.ds(pl.multiple_of(i * wide, wide), wide), :]
+            apart = dot(rows, pick, TN).astype(jnp.bfloat16)
+            for k in range(kv_count):
+                values[k, :width, pl.ds(pl.multiple_of(i * 128, 128), 128)] = apart[:, k * 128 : (k + 1) * 128]
+            return carry
+
+        lax.fori_loop(0, raw_values.shape[0] // wide, one, 0, unroll=2)
+        for k in range(kv_count):
+            values[k, width:, :] = jnp.ones((values.shape[1] - width, values.shape[2]), jnp.bfloat16)
+
+    def prepare():
+        columns = samples * group
+        row_slot = seq * slots + grid((rows_local, samples), 0) // group
+        shape = (samples, columns)
+        spread = onehot(grid(shape, 1) // group == grid(shape, 0))
+        wide = dot(onehot(slot_of[...] == row_slot), spread, NN)
+        shape = (rows_local, columns)
+        match[...] = jnp.where(grid(shape, 1) % group == grid(shape, 0) % group, wide, 0.0).astype(jnp.bfloat16)
+        shape = (group, chunk // group, chunk)
+        perm[...] = onehot(grid(shape, 2) == grid(shape, 1) * group + grid(shape, 0)).reshape(chunk, chunk)
+
     def tail(k):
         for load in tail_loads(k):
             load.wait()
-        columns = column_key.shape[1]
-        row_key = seq * rows_local + lax.broadcasted_iota(jnp.int32, (rows_local, columns), 0)
-        match = column_key[...] == row_key
-        pick = jnp.where(match, 1.0, 0.0).astype(jnp.bfloat16)
-        every = q_all[k].reshape(columns, width)
-        own_q[...] = dot(pick, every, NN)
-
-        def one(t, carry):
-            rows = pl.ds(pl.multiple_of(t * group, group), group)
+        every = q_all[k].reshape(samples * group, width)
+        own_q[...] = dot(match[...], every, NN)
+        for t in range(slots):
+            rows = slice(t * group, (t + 1) * group)
             scores = dot(own_q[rows, :].astype(jnp.bfloat16), tail_keys[k, t], NT)
-            position = lax.broadcasted_iota(jnp.int32, scores.shape, 1)
-            scores = jnp.where(position < lengths[t], scores, LOW)
-            top = jnp.max(scores, axis=1, keepdims=True)
-            weights = jnp.exp2((scores - top) * unit)
-            tail_rows[rows, :] = dot(weights.astype(jnp.bfloat16), tail_values[k, t], NN)
-            tail_m[rows, :] = jnp.broadcast_to(top, (group, width))
-            tail_l[rows, :] = jnp.broadcast_to(jnp.sum(weights, axis=1, keepdims=True), (group, width))
-            return carry
-
-        lax.fori_loop(0, slots, one, 0, unroll=4)
-        for c in range(columns // chunk):
-            span = slice(c * chunk, (c + 1) * chunk)
-            here = column_key[:, span] == row_key[:, span]
-            tail_out[c] = dot(tail_rows[...].astype(jnp.bfloat16), jnp.where(here, 1.0, 0.0).astype(jnp.bfloat16), TN)
-            top = jnp.max(jnp.where(here, tail_m[:, :1], LOW), axis=0, keepdims=True)
-            count = jnp.sum(jnp.where(here, tail_l[:, :1], 0.0), axis=0, keepdims=True)
-            tail_stat[c, 0:1] = top
-            tail_stat[c, 1:2] = count
+            tail_scores[rows, :] = jnp.where(grid(scores.shape, 1) < lengths[t], scores, LOW)
+        scores = tail_scores[...]
+        top = jnp.max(scores, axis=1, keepdims=True)
+        weights = jnp.exp2((scores - top) * unit)
+        count = jnp.sum(weights, axis=1, keepdims=True)
+        tail_scores[...] = weights
+        for t in range(slots):
+            rows = slice(t * group, (t + 1) * group)
+            tail_rows[rows, :] = dot(tail_scores[rows, :].astype(jnp.bfloat16), tail_values[k, t], NN)
+        for c in range(samples * group // chunk):
+            place = match[:, c * chunk : (c + 1) * chunk]
+            here = place.astype(jnp.float32) > 0.5
+            tail_out[c] = dot(tail_rows[...].astype(jnp.bfloat16), place, TN)
+            tail_stat[c, 0:1] = jnp.max(jnp.where(here, top, LOW), axis=0, keepdims=True)
+            tail_stat[c, 1:2] = jnp.sum(jnp.where(here, count, 0.0), axis=0, keepdims=True)
 
     def prompt(k, pair):
         q = q_all[k, pl.ds(pair * 2, 2)].reshape(2 * chunk, width)
         scores = dot(keys[k], q, NT)
         top = jnp.max(scores, axis=0, keepdims=True)
         weights = jnp.exp2((scores - top) * unit)
-        count = jnp.sum(weights, axis=0, keepdims=True)
-        rows = dot(values[k], weights.astype(jnp.bfloat16), NN)
+        both = dot(values[k], weights.astype(jnp.bfloat16), NN)
+        rows, count = both[:width], both[width : width + 1]
         for c in range(2):
             span = slice(c * chunk, (c + 1) * chunk)
             at_chunk = pair * 2 + c
@@ -348,16 +396,19 @@
                 axis=1,
             )
             first = (k * group + g) * width
-            term = dot(block, weight[first : first + 2 * width, :], NN)
+            term = dot(block, weight[:, first : first + 2 * width], NT)
             value = term if value is None else value + term
         return value
 
     a, b, c, d = order
+    prepare()
+    loads[0].wait()
+    split_keys()
     q_after_z(a)
+    loads[1].wait()
+    split_values()
+    q_after_y(a)
     q_after_z(b)
-    q_after_y(a)
-    loads[0].wait()
-    loads[1].wait()
     q_ready(a)
 
     hooks = {
@@ -426,12 +477,8 @@
     half, out_columns = samples // 2, out_weight.shape[1]
     unit = math.log2(math.e) / math.sqrt(width)
 
-    q = queries.reshape(slots, kv, group, width).transpose(1, 0, 2, 3).reshape(kv, rows, width)
-    keys = prompt_keys.transpose(1, 0, 2)
-    values = prompt_values.transpose(1, 2, 0)
-    column_key = (slot_of_sample[:, None] * group + jnp.arange(group, dtype=jnp.int32)).reshape(1, columns)
-    place = jnp.arange(chunk, dtype=jnp.int32)
-    perm = (((place % share) * group + place // share)[:, None] == place[None, :]).astype(jnp.bfloat16)
+    flat_keys = prompt_keys.reshape(positions * kv, width)
+    flat_values = prompt_values.reshape(positions * kv, width)
 
     bf16, f32 = jnp.bfloat16, jnp.float32
     vmem, hbm = pl.BlockSpec(memory_space=pltpu.VMEM), pl.BlockSpec(memory_space=pl.ANY)
@@ -439,18 +486,22 @@
     return pl.pallas_call(
         functools.partial(kernel, unit),
         out_shape=jax.ShapeDtypeStruct((half, out_columns), f32),
-        in_specs=[vmem, hbm, hbm, hbm, hbm, pl.BlockSpec(memory_space=pltpu.SMEM), vmem, vmem, hbm],
+        in_specs=[vmem, hbm, hbm, hbm, hbm, pl.BlockSpec(memory_space=pltpu.SMEM), vmem, hbm],
         out_specs=vmem,
         scratch_shapes=[
+            pltpu.VMEM((kv, rows, width), bf16),
+            pltpu.VMEM(flat_keys.shape, bf16),
+            pltpu.VMEM(flat_values.shape, bf16),
+            pltpu.VMEM((chunk, chunk), bf16),
+            pltpu.VMEM((rows, columns), bf16),
             pltpu.VMEM((kv, ZS, YS, CS, rows, width), bf16),
-            pltpu.VMEM(keys.shape, bf16),
-            pltpu.VMEM(values.shape, bf16),
+            pltpu.VMEM((kv, positions, width), bf16),
+            pltpu.VMEM((kv, width + 16, positions), bf16),
             pltpu.VMEM((kv, slots, tail_len, width), bf16),
             pltpu.VMEM((kv, slots, tail_len, width), bf16),
-            pltpu.VMEM(out_weight.shape, bf16),
+            pltpu.VMEM(out_weight.shape[::-1], bf16),
             pltpu.VMEM((rows, width), f32),
-            pltpu.VMEM((rows, width), f32),
-            pltpu.VMEM((rows, width), f32),
+            pltpu.VMEM((rows, tail_len), f32),
             pltpu.VMEM((rows, width), f32),
             pltpu.VMEM((ZS, width, chunk), f32),
             pltpu.VMEM((ZS, 8, chunk), f32),
@@ -489,7 +540,16 @@
         compiler_params=pltpu.CompilerParams(
             collective_id=0, has_side_effects=True, vmem_limit_bytes=62 * 1024 * 1024
         ),
-    )(q, keys, values, suffix_keys, suffix_values, suffix_lengths, column_key, perm, out_weight)
+    )(
+        queries,
+        flat_keys,
+        flat_values,
+        suffix_keys,
+        suffix_values,
+        suffix_lengths,
+        slot_of_sample.reshape(1, samples),
+        out_weight.T,
+    )
 
 
 def partial_softmax(scores, values_block, equation):

time: 114 us -> 92.6 us (0.81)
  local copies, waits for them, and re-layouts: 13.5 us -> 1.58 us
  Pallas kernels: 98.5 us -> 90.9 us
  other arithmetic: 1.64 us -> 0 us
    unnamed x8 -> x1, local copies, waits for them, and re-layouts: 12.1 us -> 1.58 us
    pallas_call x1, Pallas kernels: 98.5 us -> 90.9 us  [fused(): pl.pallas_call(functools.partial(kernel, unit), out_shape=jax.ShapeDtypeS...]
where the time goes in v2:
time: 92.6 us; the launch traced here: 92.5 us
  Pallas kernels  90.9 us (98%)
  local copies, waits for them, and re-layouts  1.58 us (2%)
    pallas_call x1, Pallas kernels, fused(): pl.pallas_call(functools.partial(kernel, unit), out_shape=jax.ShapeDtypeS...  90.9 us

profile of v2, /device:TPU:0, one launch (start us, length us, event | category | flops | bytes accessed | tf_op | source)
XLA Modules:
  0.0 92.5 jit_solution(12656030848796310089)
XLA Ops:
  0.0 90.9 %shard_map.82 = f32[96,320]{1,0:T(8,128)} custom-call(bf16[12,32,128]{2,1,0:T(8,128)(2,1)} %q_in.1, bf16[8192,128]{1,0:T(8,128)(2,1)} %bitcast.5, bf16[8192,128]{1,0:T(8,128)(2,1)} %bitcast.6, bf16[12,4,1024,128]{3,2,1,0:T(8,128)(2,1)} %tail_keys_in.1, bf16[12,4,1024,128]{3,2,1,0:T(8,128)(2,1)} %tail_values_in.1, s32[12]{0:T(128)} %lengths.1, ...), custom_call_target="tpu_custom_call" | custom-call | tf_op jit(solution)/shard_map/pallas_call | solution.py:486
  90.9 1.6 %copy.10 = f32[96,320]{1,0:T(8,128)} copy(f32[96,320]{1,0:T(8,128)} %shard_map.82) | data formatting | bytes 245760

commit v3 on v2

--- a/solution.py
+++ b/solution.py
@@ -84,7 +84,6 @@
     y_sems,
     zs_send,
     zs_recv,
-    zo_sems,
     az_send,
     az_recv,
     a_sems,
@@ -95,6 +94,9 @@
     group = rows_local // slots
     samples = slot_of.shape[1]
     chunk = YS * CS * rows_local
+    lanes = part.shape[-1]
+    thirds = chunk // lanes
+    units = kv_count * thirds
     seq, head = lax.axis_index("seq"), lax.axis_index("head")
     z, y, core = seq // (YS * CS), (seq // CS) % YS, seq % CS
     other_y, other_core, other_head = 1 - y, 1 - core, 1 - head
@@ -148,25 +150,36 @@
         pl.semaphore_signal(barrier, inc=1, device_id=peer, device_id_type=MESH)
     pl.semaphore_wait(barrier, len(peers))
 
+    def block(y_of, core_of):
+        return pl.ds((y_of * CS + core_of) * rows_local, rows_local)
+
     def q_z(k):
         return [
-            remote(q_own.at[k], q_all.at[k, z, y, core], qz_send_sem.at[k, i], qz_recv_sem.at[k, i], z_peers[i])
+            remote(q_own.at[k], q_all.at[k, z, block(y, core)], qz_send_sem.at[k, i], qz_recv_sem.at[k, i], z_peers[i])
             for i in range(ZS - 1)
         ]
 
     def q_y(k):
-        mine = q_all.at[k, :, y, core]
+        mine = q_all.at[k, :, block(y, core)]
         return remote(mine, mine, q_sems.at[k, 0], q_sems.at[k, 1], y_peer)
 
     def q_core(k):
-        mine = q_all.at[k, :, :, core]
-        return remote(mine, mine, q_sems.at[k, 2], q_sems.at[k, 3], core_peer)
+        return [
+            remote(
+                q_all.at[k, :, block(i, core)],
+                q_all.at[k, :, block(i, core)],
+                q_sems.at[k, 2 + 2 * i],
+                q_sems.at[k, 3 + 2 * i],
+                core_peer,
+            )
+            for i in range(YS)
+        ]
 
     for k in order:
         for copy in q_z(k):
             copy.start()
     for k in order:
-        q_all[k, z, y, core] = q_own[k]
+        q_all[k, z, block(y, core), :] = q_own[k]
 
     def q_after_z(k):
         for copy in q_z(k):
@@ -175,10 +188,12 @@
 
     def q_after_y(k):
         q_y(k).wait()
-        q_core(k).start()
+        for copy in q_core(k):
+            copy.start()
 
     def q_ready(k):
-        q_core(k).wait()
+        for copy in q_core(k):
+            copy.wait()
 
     def split_keys():
         size = 256 // kv_count
@@ -218,8 +233,8 @@
         wide = dot(onehot(slot_of[...] == row_slot), spread, NN)
         shape = (rows_local, columns)
         match[...] = jnp.where(grid(shape, 1) % group == grid(shape, 0) % group, wide, 0.0).astype(jnp.bfloat16)
-        shape = (group, chunk // group, chunk)
-        perm[...] = onehot(grid(shape, 2) == grid(shape, 1) * group + grid(shape, 0)).reshape(chunk, chunk)
+        shape = (group, lanes // group, lanes)
+        perm[...] = onehot(grid(shape, 2) == grid(shape, 1) * group + grid(shape, 0)).reshape(lanes, lanes)
 
     def tail(k):
         for load in tail_loads(k):
@@ -241,164 +256,197 @@
         for c in range(samples * group // chunk):
             place = match[:, c * chunk : (c + 1) * chunk]
             here = place.astype(jnp.float32) > 0.5
-            tail_out[c] = dot(tail_rows[...].astype(jnp.bfloat16), place, TN)
-            tail_stat[c, 0:1] = jnp.max(jnp.where(here, top, LOW), axis=0, keepdims=True)
-            tail_stat[c, 1:2] = jnp.sum(jnp.where(here, count, 0.0), axis=0, keepdims=True)
-
-    def prompt(k, pair):
-        q = q_all[k, pl.ds(pair * 2, 2)].reshape(2 * chunk, width)
-        scores = dot(keys[k], q, NT)
-        top = jnp.max(scores, axis=0, keepdims=True)
-        weights = jnp.exp2((scores - top) * unit)
-        both = dot(values[k], weights.astype(jnp.bfloat16), NN)
-        rows, count = both[:width], both[width : width + 1]
-        for c in range(2):
-            span = slice(c * chunk, (c + 1) * chunk)
-            at_chunk = pair * 2 + c
-            o, m, l = merge(
+            rows = dot(tail_rows[...].astype(jnp.bfloat16), place, TN)
+            best = jnp.max(jnp.where(here, top, LOW), axis=0, keepdims=True)
+            sums = jnp.sum(jnp.where(here, count, 0.0), axis=0, keepdims=True)
+            for r in range(thirds):
+                span = slice(r * lanes, (r + 1) * lanes)
+                tail_out[r, c] = rows[:, span]
+                tail_stat[r, c, 0:1] = best[:, span]
+                tail_stat[r, c, 1:2] = sums[:, span]
+
+    def prompt(u, k, r):
+        q = q_all[k, :, pl.ds(pl.multiple_of(r * lanes, lanes), lanes), :]
+        pairs = ZS // 2
+        scores = [dot(keys[k], q[2 * p : 2 * p + 2].reshape(2 * lanes, width), NT) for p in range(pairs)]
+        for p in range(pairs):
+            top = jnp.max(scores[p], axis=0, keepdims=True)
+            weights = jnp.exp2((scores[p] - top) * unit).astype(jnp.bfloat16)
+            both = dot(values[k], weights, NN)
+            for c in range(2):
+                span = slice(c * lanes, (c + 1) * lanes)
+                at_chunk = p * 2 + c
+                o, m, l = merge(
+                    [
+                        (both[:width, span], top[:, span], both[width : width + 1, span]),
+                        (tail_out[r, at_chunk], tail_stat[r, at_chunk, 0:1], tail_stat[r, at_chunk, 1:2]),
+                    ],
+                    unit,
+                )
+                part[u, p, c] = o.astype(jnp.bfloat16)
+                stat[u, p, c, 0:1] = m
+                stat[u, p, c, 1:2] = l
+
+    def sum_core(u):
+        return [
+            remote(part.at[u, :, other_core], core_part.at[u], core_sems.at[u, 0], core_sems.at[u, 1], core_peer),
+            remote(stat.at[u, :, other_core], core_stat.at[u], core_sems.at[u, 2], core_sems.at[u, 3], core_peer),
+        ]
+
+    def sum_y(u):
+        return [
+            remote(y_send.at[u], y_part.at[u], y_sems.at[u, 0], y_sems.at[u, 1], y_peer),
+            remote(y_send_stat.at[u], y_stat.at[u], y_sems.at[u, 2], y_sems.at[u, 3], y_peer),
+        ]
+
+    def head_of(u):
+        return (3 * (u // thirds)) % kv_count
+
+    def sum_z_out(u):
+        k, r = head_of(u), u % thirds
+        slot = (z - k + 2 * ZS - 1) % ZS
+        return [
+            remote(z_send.at[u], z_part.at[r, slot], zs_send.at[u, 0], zs_recv.at[r, slot, 0], at(k, y, core)),
+            remote(z_send_stat.at[u], z_stat.at[r, slot], zs_send.at[u, 1], zs_recv.at[r, slot, 1], at(k, y, core)),
+        ]
+
+    def sum_z_in(u, slot):
+        r = u % thirds
+        return [
+            remote(z_send.at[u], z_part.at[r, slot], zs_send.at[u, 0], zs_recv.at[r, slot, 0], y_peer),
+            remote(z_send_stat.at[u], z_stat.at[r, slot], zs_send.at[u, 1], zs_recv.at[r, slot, 1], y_peer),
+        ]
+
+    def att_z(u, i):
+        mine = att.at[u, y, core]
+        return remote(mine, mine, az_send.at[u, i], az_recv.at[u], z_peers[i])
+
+    def att_y(u):
+        mine = att.at[u, y, core]
+        return remote(mine, mine, a_sems.at[u, 0], a_sems.at[u, 1], y_peer)
+
+    def att_core(u):
+        mine = att.at[u, :, core]
+        return remote(mine, mine, a_sems.at[u, 2], a_sems.at[u, 3], core_peer)
+
+    def swap(r):
+        rows = pl.ds(r * (lanes // group), lanes // group)
+        return remote(
+            total.at[pl.ds(2 * other_head, 2), rows],
+            x_part.at[:, rows],
+            x_sems.at[r, 0],
+            x_sems.at[r, 1],
+            x_peer,
+        )
+
+    def step_a(u):
+        for copy in sum_core(u):
+            copy.start()
+
+    def step_b(u):
+        for copy in sum_core(u):
+            copy.wait()
+
+        def joined(i):
+            return merge(
                 [
-                    (rows[:, span], top[:, span], count[:, span]),
-                    (tail_out[at_chunk], tail_stat[at_chunk, 0:1], tail_stat[at_chunk, 1:2]),
+                    (part[u, i, core].astype(jnp.float32), stat[u, i, core, 0:1], stat[u, i, core, 1:2]),
+                    (core_part[u, i].astype(jnp.float32), core_stat[u, i, 0:1], core_stat[u, i, 1:2]),
                 ],
                 unit,
             )
-            part[k, pair, c] = o.astype(jnp.bfloat16)
-            stat[k, pair, c, 0:1] = m
-            stat[k, pair, c, 1:2] = l
-
-    def sum_core(k):
-        return [
-            remote(part.at[k, :, other_core], core_part.at[k], core_sems.at[k, 0], core_sems.at[k, 1], core_peer),
-            remote(stat.at[k, :, other_core], core_stat.at[k], core_sems.at[k, 2], core_sems.at[k, 3], core_peer),
-        ]
-
-    def sum_y(k):
-        return [
-            remote(y_send.at[k], y_part.at[k], y_sems.at[k, 0], y_sems.at[k, 1], y_peer),
-            remote(y_send_stat.at[k], y_stat.at[k], y_sems.at[k, 2], y_sems.at[k, 3], y_peer),
-        ]
-
-    def sum_z(k):
-        slot = (z - k + ZS - 1) % ZS
-        return [
-            remote(z_send.at[k], z_part.at[slot], zs_send.at[k, 0], zs_recv.at[slot, 0], at(k, y, core)),
-            remote(z_send_stat.at[k], z_stat.at[slot], zs_send.at[k, 1], zs_recv.at[slot, 1], at(k, y, core)),
-        ]
-
-    def att_z(k):
-        mine = att.at[k, y, core]
-        return [
-            remote(mine, mine, az_send.at[i], az_recv.at[k], at((k + 1 + i) % ZS, y, core)) for i in range(ZS - 1)
-        ]
-
-    def att_y(k):
-        mine = att.at[k, y, core]
-        return remote(mine, mine, a_sems.at[k, 0], a_sems.at[k, 1], y_peer)
-
-    def att_core(k):
-        mine = att.at[k, :, core]
-        return remote(mine, mine, a_sems.at[k, 2], a_sems.at[k, 3], core_peer)
-
-    def step_a(k):
-        for copy in sum_core(k):
-            copy.start()
-
-    def step_b(k):
-        for copy in sum_core(k):
-            copy.wait()
-
-        def joined(i):
-            return merge(
-                [
-                    (part[k, i, core].astype(jnp.float32), stat[k, i, core, 0:1], stat[k, i, core, 1:2]),
-                    (core_part[k, i].astype(jnp.float32), core_stat[k, i, 0:1], core_stat[k, i, 1:2]),
-                ],
-                unit,
-            )
 
         o, m, l = joined(other_y)
-        y_send[k] = o.astype(jnp.bfloat16)
-        y_send_stat[k, 0:1] = m
-        y_send_stat[k, 1:2] = l
-        for copy in sum_y(k):
+        y_send[u] = o.astype(jnp.bfloat16)
+        y_send_stat[u, 0:1] = m
+        y_send_stat[u, 1:2] = l
+        for copy in sum_y(u):
             copy.start()
         o, m, l = joined(y)
-        y_own[k] = o
-        y_own_stat[k, 0:1] = m
-        y_own_stat[k, 1:2] = l
-
-    def step_c(k):
-        for copy in sum_y(k):
+        y_own[u] = o
+        y_own_stat[u, 0:1] = m
+        y_own_stat[u, 1:2] = l
+
+    def step_c(u):
+        for copy in sum_y(u):
             copy.wait()
         o, m, l = merge(
             [
-                (y_own[k], y_own_stat[k, 0:1], y_own_stat[k, 1:2]),
-                (y_part[k].astype(jnp.float32), y_stat[k, 0:1], y_stat[k, 1:2]),
+                (y_own[u], y_own_stat[u, 0:1], y_own_stat[u, 1:2]),
+                (y_part[u].astype(jnp.float32), y_stat[u, 0:1], y_stat[u, 1:2]),
             ],
             unit,
         )
-        y_own[k] = o
-        z_send[k] = o.astype(jnp.bfloat16)
-        z_send_stat[k, 0:1] = m
-        z_send_stat[k, 1:2] = l
-
-        @pl.when(z != k)
+        y_own[u] = o
+        z_send[u] = o.astype(jnp.bfloat16)
+        z_send_stat[u, 0:1] = m
+        z_send_stat[u, 1:2] = l
+
+        @pl.when(z != head_of(u))
         def _():
-            for copy in sum_z(k):
+            for copy in sum_z_out(u):
                 copy.start()
 
-    def step_d(k):
-        @pl.when(z != k)
+    def step_d(u):
+        @pl.when(z != head_of(u))
         def _():
-            for copy in sum_z(k):
+            for copy in sum_z_out(u):
                 copy.wait_send()
 
-        @pl.when(z == k)
+        @pl.when(z == head_of(u))
         def _():
-            parts = [(y_own[k], z_send_stat[k, 0:1], z_send_stat[k, 1:2])]
+            parts = [(y_own[u], z_send_stat[u, 0:1], z_send_stat[u, 1:2])]
+            r = u % thirds
             for slot in range(ZS - 1):
-                device = at(k, y, core)
-                remote(z_send.at[k], z_part.at[slot], zs_send.at[k, 0], zs_recv.at[slot, 0], device).wait_recv()
-                remote(z_send_stat.at[k], z_stat.at[slot], zs_send.at[k, 1], zs_recv.at[slot, 1], device).wait_recv()
-                parts.append((z_part[slot].astype(jnp.float32), z_stat[slot, 0:1], z_stat[slot, 1:2]))
+                for copy in sum_z_in(u, slot):
+                    copy.wait_recv()
+                parts.append((z_part[r, slot].astype(jnp.float32), z_stat[r, slot, 0:1], z_stat[r, slot, 1:2]))
             o, _, l = merge(parts, unit)
             attention = (o / l).astype(jnp.bfloat16)
             rows = dot(perm[...], attention, NT).astype(jnp.bfloat16)
-            att[k, y, core] = rows.reshape(att.shape[3:])
-            for copy in att_z(k):
-                copy.start()
-
-    def step_e(k):
-        @pl.when(z != k)
+            att[u, y, core] = rows.reshape(att.shape[3:])
+            for i in range(ZS - 1):
+                att_z(u, i).start()
+
+    def step_e(u):
+        @pl.when(z != head_of(u))
         def _():
-            att_z(k)[0].wait_recv()
-
-        att_y(k).start()
-
-    def step_f(k):
-        @pl.when(z == k)
+            att_z(u, 0).wait_recv()
+
+        att_y(u).start()
+
+    def step_f(u):
+        @pl.when(z == head_of(u))
         def _():
-            for copy in att_z(k):
-                copy.wait_send()
-
-        att_y(k).wait()
-        att_core(k).start()
-
-    def step_g(k):
-        att_core(k).wait()
+            for i in range(ZS - 1):
+                att_z(u, i).wait_send()
+
+        att_y(u).wait()
+        att_core(u).start()
+
+    def step_g(u):
+        att_core(u).wait()
+        k, r = head_of(u), u % thirds
         value = None
         for g in range(0, group, 2):
-            block = jnp.concatenate(
+            rows = jnp.concatenate(
                 [
-                    jnp.concatenate([att[k, i, j, g + h] for i in range(YS) for j in range(CS)], axis=0)
+                    jnp.concatenate([att[u, i, j, g + h] for i in range(YS) for j in range(CS)], axis=0)
                     for h in range(2)
                 ],
                 axis=1,
             )
-            first = (k * group + g) * width
-            term = dot(block, weight[:, first : first + 2 * width], NT)
+            first = pl.multiple_of((k * group + g) * width, 2 * width)
+            term = dot(rows, weight[:, pl.ds(first, 2 * width)], NT)
             value = term if value is None else value + term
-        return value
+        count = lanes // group
+        rows = pl.ds(pl.multiple_of(r * count, count), count)
+        for c in range(ZS):
+            total[c, rows, :] += value[c * count : (c + 1) * count]
+
+        @pl.when(u >= units - thirds)
+        def _():
+            swap(r).start()
 
     a, b, c, d = order
     prepare()
@@ -411,26 +459,36 @@
     q_after_z(b)
     q_ready(a)
 
-    hooks = {
+    total[...] = jnp.zeros_like(total)
+    loads[2].wait()
+    q_hooks = {
         0: [(q_after_z, c), (q_after_y, b)],
-        1: [(step_a, a), (q_after_z, d), (q_after_y, c), (q_ready, b)],
-        2: [(step_b, a), (q_after_y, d)],
-        3: [(step_c, a), (step_a, b), (q_ready, c)],
-        4: [(step_d, a), (step_b, b)],
-        5: [(step_e, a), (step_c, b), (step_a, c), (q_ready, d)],
-        6: [(step_f, a), (step_d, b), (step_b, c)],
-        7: [(step_a, d), (step_e, b), (step_c, c)],
+        1: [(q_after_z, d)],
+        2: [(q_ready, b), (q_after_y, c)],
+        3: [(q_after_y, d)],
+        5: [(q_ready, c)],
+        8: [(q_ready, d)],
     }
+    stages = [step_a, step_b, step_c, step_d, step_e, step_f, step_g]
 
     def turn(i, carry):
-        k, pair = (3 * (i // 2)) % kv_count, i % 2
-
-        @pl.when(pair == 0)
+        @pl.when(i < units)
         def _():
-            tail(k)
-
-        prompt(k, pair)
-        for at_turn, calls in hooks.items():
+            k, r = head_of(i), i % thirds
+
+            @pl.when(r == 0)
+            def _():
+                tail(k)
+
+            prompt(i, k, r)
+
+        for late in reversed(range(len(stages))):
+
+            @pl.when((i >= late) & (i < units + late))
+            def _(late=late):
+                stages[late](i - late)
+
+        for at_turn, calls in q_hooks.items():
 
             @pl.when(i == at_turn)
             def _(calls=calls):
@@ -439,28 +497,10 @@
 
         return carry
 
-    lax.fori_loop(0, 2 * kv_count, turn, 0)
-    step_b(d)
-    step_d(c)
-    step_f(b)
-    step_c(d)
-    loads[2].wait()
-    value = step_g(a)
-    step_e(c)
-    step_d(d)
-    value += step_g(b)
-    step_f(c)
-    step_e(d)
-    value += step_g(c)
-    step_f(d)
-    value += step_g(d)
-    half = value.shape[0] // 2
-    total[0] = value[:half]
-    total[1] = value[half:]
-    swap = remote(total.at[other_head], x_part, x_sems.at[0], x_sems.at[1], x_peer)
-    swap.start()
-    swap.wait()
-    out[...] = total[head] + x_part[...]
+    lax.fori_loop(0, units + len(stages) - 1, turn, 0)
+    for r in range(thirds):
+        swap(r).wait()
+    out[...] = (total[pl.ds(2 * head, 2)] + x_part[...]).reshape(out.shape)
 
 
 def fused(queries, prompt_keys, prompt_values, suffix_keys, suffix_values, suffix_lengths, slot_of_sample, out_weight):
@@ -472,7 +512,9 @@
     samples = slot_of_sample.shape[0]
     columns = samples * group
     chunk = YS * CS * rows
-    share = chunk // group
+    lanes = 128
+    thirds = chunk // lanes
+    units = kv * thirds
     tail_len = suffix_keys.shape[2]
     half, out_columns = samples // 2, out_weight.shape[1]
     unit = math.log2(math.e) / math.sqrt(width)
@@ -492,9 +534,9 @@
             pltpu.VMEM((kv, rows, width), bf16),
             pltpu.VMEM(flat_keys.shape, bf16),
             pltpu.VMEM(flat_values.shape, bf16),
-            pltpu.VMEM((chunk, chunk), bf16),
+            pltpu.VMEM((lanes, lanes), bf16),
             pltpu.VMEM((rows, columns), bf16),
-            pltpu.VMEM((kv, ZS, YS, CS, rows, width), bf16),
+            pltpu.VMEM((kv, ZS, chunk, width), bf16),
             pltpu.VMEM((kv, positions, width), bf16),
             pltpu.VMEM((kv, width + 16, positions), bf16),
             pltpu.VMEM((kv, slots, tail_len, width), bf16),
@@ -503,39 +545,38 @@
             pltpu.VMEM((rows, width), f32),
             pltpu.VMEM((rows, tail_len), f32),
             pltpu.VMEM((rows, width), f32),
-            pltpu.VMEM((ZS, width, chunk), f32),
-            pltpu.VMEM((ZS, 8, chunk), f32),
-            pltpu.VMEM((kv, YS, CS, width, chunk), bf16),
-            pltpu.VMEM((kv, YS, CS, 8, chunk), f32),
-            pltpu.VMEM((kv, YS, width, chunk), bf16),
-            pltpu.VMEM((kv, YS, 8, chunk), f32),
-            pltpu.VMEM((kv, width, chunk), f32),
-            pltpu.VMEM((kv, width, chunk), bf16),
-            pltpu.VMEM((kv, width, chunk), bf16),
-            pltpu.VMEM((kv, 8, chunk), f32),
-            pltpu.VMEM((kv, 8, chunk), f32),
-            pltpu.VMEM((kv, 8, chunk), f32),
-            pltpu.VMEM((kv, width, chunk), bf16),
-            pltpu.VMEM((kv, 8, chunk), f32),
-            pltpu.VMEM((ZS - 1, width, chunk), bf16),
-            pltpu.VMEM((ZS - 1, 8, chunk), f32),
-            pltpu.VMEM((kv, YS, CS, group, share, width), bf16),
-            pltpu.VMEM((2, half, out_columns), f32),
-            pltpu.VMEM((half, out_columns), f32),
+            pltpu.VMEM((thirds, ZS, width, lanes), f32),
+            pltpu.VMEM((thirds, ZS, 8, lanes), f32),
+            pltpu.VMEM((units, YS, CS, width, lanes), bf16),
+            pltpu.VMEM((units, YS, CS, 8, lanes), f32),
+            pltpu.VMEM((units, YS, width, lanes), bf16),
+            pltpu.VMEM((units, YS, 8, lanes), f32),
+            pltpu.VMEM((units, width, lanes), f32),
+            pltpu.VMEM((units, width, lanes), bf16),
+            pltpu.VMEM((units, width, lanes), bf16),
+            pltpu.VMEM((units, 8, lanes), f32),
+            pltpu.VMEM((units, 8, lanes), f32),
+            pltpu.VMEM((units, 8, lanes), f32),
+            pltpu.VMEM((units, width, lanes), bf16),
+            pltpu.VMEM((units, 8, lanes), f32),
+            pltpu.VMEM((thirds, ZS - 1, width, lanes), bf16),
+            pltpu.VMEM((thirds, ZS - 1, 8, lanes), f32),
+            pltpu.VMEM((units, YS, CS, group, lanes // group, width), bf16),
+            pltpu.VMEM((ZS, samples // ZS, out_columns), f32),
+            pltpu.VMEM((2, samples // ZS, out_columns), f32),
             sem((3,)),
             sem((kv, 2)),
-            sem((kv, 4)),
+            sem((kv, 6)),
             sem((kv, ZS - 1)),
             sem((kv, ZS - 1)),
-            sem((kv, 4)),
-            sem((kv, 4)),
-            sem((kv, 2)),
-            sem((ZS - 1, 2)),
-            sem((1,)),
-            sem((ZS - 1,)),
-            sem((kv,)),
-            sem((kv, 4)),
-            sem((2,)),
+            sem((units, 4)),
+            sem((units, 4)),
+            sem((units, 2)),
+            sem((thirds, ZS - 1, 2)),
+            sem((units, ZS - 1)),
+            sem((units,)),
+            sem((units, 4)),
+            sem((thirds, 2)),
         ],
         compiler_params=pltpu.CompilerParams(
             collective_id=0, has_side_effects=True, vmem_limit_bytes=62 * 1024 * 1024

time: 92.6 us -> 93.2 us (level)
  no operation moved by 1% of the time
where the time goes in v3:
time: 93.2 us; the launch traced here: 93.1 us
  Pallas kernels  91.5 us (98%)
  local copies, waits for them, and re-layouts  1.58 us (2%)
    pallas_call x1, Pallas kernels, fused(): pl.pallas_call(functools.partial(kernel, unit), out_shape=jax.ShapeDtypeS...  91.5 us

profile of v3, /device:TPU:0, one launch (start us, length us, event | category | flops | bytes accessed | tf_op | source)
XLA Modules:
  0.0 93.1 jit_solution(17873083158192429214)
XLA Ops:
  0.0 91.5 %shard_map.82 = f32[96,320]{1,0:T(8,128)} custom-call(bf16[12,32,128]{2,1,0:T(8,128)(2,1)} %q_in.1, bf16[8192,128]{1,0:T(8,128)(2,1)} %bitcast.5, bf16[8192,128]{1,0:T(8,128)(2,1)} %bitcast.6, bf16[12,4,1024,128]{3,2,1,0:T(8,128)(2,1)} %tail_keys_in.1, bf16[12,4,1024,128]{3,2,1,0:T(8,128)(2,1)} %tail_values_in.1, s32[12]{0:T(128)} %lengths.1, ...), custom_call_target="tpu_custom_call" | custom-call | tf_op jit(solution)/shard_map/pallas_call | solution.py:528
  91.5 1.6 %copy.10 = f32[96,320]{1,0:T(8,128)} copy(f32[96,320]{1,0:T(8,128)} %shard_map.82) | data formatting | bytes 245760

commit v4 on v3

--- a/solution.py
+++ b/solution.py
@@ -58,6 +58,14 @@
     tail_rows,
     tail_out,
     tail_stat,
+    scores_a,
+    scores_b,
+    weights_b,
+    out_a,
+    out_b,
+    top_a,
+    top_b,
+    top_last,
     part,
     stat,
     core_part,
@@ -175,11 +183,14 @@
             for i in range(YS)
         ]
 
+    for copy in q_z(order[0]):
+        copy.start()
     for k in order:
+        q_all[k, z, block(y, core), :] = q_own[k]
+
+    def q_start(k):
         for copy in q_z(k):
             copy.start()
-    for k in order:
-        q_all[k, z, block(y, core), :] = q_own[k]
 
     def q_after_z(k):
         for copy in q_z(k):
@@ -236,7 +247,7 @@
         shape = (group, lanes // group, lanes)
         perm[...] = onehot(grid(shape, 2) == grid(shape, 1) * group + grid(shape, 0)).reshape(lanes, lanes)
 
-    def tail(k):
+    def tail(k, base):
         for load in tail_loads(k):
             load.wait()
         every = q_all[k].reshape(samples * group, width)
@@ -261,31 +272,49 @@
             sums = jnp.sum(jnp.where(here, count, 0.0), axis=0, keepdims=True)
             for r in range(thirds):
                 span = slice(r * lanes, (r + 1) * lanes)
-                tail_out[r, c] = rows[:, span]
-                tail_stat[r, c, 0:1] = best[:, span]
-                tail_stat[r, c, 1:2] = sums[:, span]
-
-    def prompt(u, k, r):
-        q = q_all[k, :, pl.ds(pl.multiple_of(r * lanes, lanes), lanes), :]
-        pairs = ZS // 2
-        scores = [dot(keys[k], q[2 * p : 2 * p + 2].reshape(2 * lanes, width), NT) for p in range(pairs)]
-        for p in range(pairs):
-            top = jnp.max(scores[p], axis=0, keepdims=True)
-            weights = jnp.exp2((scores[p] - top) * unit).astype(jnp.bfloat16)
-            both = dot(values[k], weights, NN)
-            for c in range(2):
-                span = slice(c * lanes, (c + 1) * lanes)
-                at_chunk = p * 2 + c
-                o, m, l = merge(
-                    [
-                        (both[:width, span], top[:, span], both[width : width + 1, span]),
-                        (tail_out[r, at_chunk], tail_stat[r, at_chunk, 0:1], tail_stat[r, at_chunk, 1:2]),
-                    ],
-                    unit,
-                )
-                part[u, p, c] = o.astype(jnp.bfloat16)
-                stat[u, p, c, 0:1] = m
-                stat[u, p, c, 1:2] = l
+                tail_out[base + r, c] = rows[:, span]
+                tail_stat[base + r, c, 0:1] = best[:, span]
+                tail_stat[base + r, c, 1:2] = sums[:, span]
+
+    def scores_of(u, pair):
+        k, r = head_of(u), u % thirds
+        q = q_all[k, 2 * pair : 2 * pair + 2, pl.ds(pl.multiple_of(r * lanes, lanes), lanes), :]
+        return dot(keys[k], q.reshape(2 * lanes, width), NT)
+
+    def softmax(scores_ref, top_ref):
+        scores = scores_ref[...]
+        top = jnp.max(scores, axis=0, keepdims=True)
+        top_ref[0:1] = top
+        return jnp.exp2((scores - top) * unit).astype(jnp.bfloat16)
+
+    def prompt(u):
+        before, after = jnp.maximum(u - 1, 0), jnp.minimum(u + 1, units - 1)
+        scores_b[...] = scores_of(u, 1)
+        weights = softmax(scores_a, top_a)
+        out_b[...] = dot(values[head_of(before)], weights_b[...], NN)
+        top_last[...] = top_b[...]
+        scores_a[...] = scores_of(after, 0)
+        weights_b[...] = softmax(scores_b, top_b)
+        out_a[...] = dot(values[head_of(u)], weights, NN)
+
+    def prompt_last():
+        out_b[...] = dot(values[head_of(units - 1)], weights_b[...], NN)
+        top_last[...] = top_b[...]
+
+    def store(u, pair, both, top, tails, tail_stats):
+        for c in range(2):
+            span = slice(c * lanes, (c + 1) * lanes)
+            at_chunk = pair * 2 + c
+            o, m, l = merge(
+                [
+                    (both[:width, span], top[0:1, span], both[width : width + 1, span]),
+                    (tails[at_chunk], tail_stats[at_chunk, 0:1], tail_stats[at_chunk, 1:2]),
+                ],
+                unit,
+            )
+            part[u, pair, c] = o.astype(jnp.bfloat16)
+            stat[u, pair, c, 0:1] = m
+            stat[u, pair, c, 1:2] = l
 
     def sum_core(u):
         return [
@@ -329,17 +358,12 @@
         mine = att.at[u, :, core]
         return remote(mine, mine, a_sems.at[u, 2], a_sems.at[u, 3], core_peer)
 
-    def swap(r):
-        rows = pl.ds(r * (lanes // group), lanes // group)
-        return remote(
-            total.at[pl.ds(2 * other_head, 2), rows],
-            x_part.at[:, rows],
-            x_sems.at[r, 0],
-            x_sems.at[r, 1],
-            x_peer,
-        )
+    def swap():
+        return remote(total.at[pl.ds(2 * other_head, 2)], x_part, x_sems.at[0], x_sems.at[1], x_peer)
 
     def step_a(u):
+        kept = ((u // thirds) % 2) * thirds + u % thirds
+        store(u, 1, out_b, top_last, tail_out.at[kept], tail_stat.at[kept])
         for copy in sum_core(u):
             copy.start()
 
@@ -426,12 +450,26 @@
 
     def step_g(u):
         att_core(u).wait()
-        k, r = head_of(u), u % thirds
+
+        @pl.when(u % thirds == thirds - 1)
+        def _():
+            project(u // thirds)
+
+    def project(turn_of):
+        k = (3 * turn_of) % kv_count
         value = None
         for g in range(0, group, 2):
             rows = jnp.concatenate(
                 [
-                    jnp.concatenate([att[u, i, j, g + h] for i in range(YS) for j in range(CS)], axis=0)
+                    jnp.concatenate(
+                        [
+                            att[turn_of * thirds + r, i, j, g + h]
+                            for i in range(YS)
+                            for j in range(CS)
+                            for r in range(thirds)
+                        ],
+                        axis=0,
+                    )
                     for h in range(2)
                 ],
                 axis=1,
@@ -439,35 +477,31 @@
             first = pl.multiple_of((k * group + g) * width, 2 * width)
             term = dot(rows, weight[:, pl.ds(first, 2 * width)], NT)
             value = term if value is None else value + term
-        count = lanes // group
-        rows = pl.ds(pl.multiple_of(r * count, count), count)
-        for c in range(ZS):
-            total[c, rows, :] += value[c * count : (c + 1) * count]
-
-        @pl.when(u >= units - thirds)
-        def _():
-            swap(r).start()
+        total[...] += value.reshape(total.shape)
 
     a, b, c, d = order
     prepare()
     loads[0].wait()
     split_keys()
     q_after_z(a)
+    q_start(b)
     loads[1].wait()
     split_values()
     q_after_y(a)
-    q_after_z(b)
+    q_start(c)
+    q_start(d)
     q_ready(a)
+    scores_a[...] = scores_of(0, 0)
 
     total[...] = jnp.zeros_like(total)
     loads[2].wait()
     q_hooks = {
-        0: [(q_after_z, c), (q_after_y, b)],
-        1: [(q_after_z, d)],
-        2: [(q_ready, b), (q_after_y, c)],
+        0: [(q_after_z, b), (q_after_z, c)],
+        1: [(q_after_y, b), (q_ready, b), (q_after_z, d)],
+        2: [(q_after_y, c)],
         3: [(q_after_y, d)],
-        5: [(q_ready, c)],
-        8: [(q_ready, d)],
+        4: [(q_ready, c)],
+        7: [(q_ready, d)],
     }
     stages = [step_a, step_b, step_c, step_d, step_e, step_f, step_g]
 
@@ -478,15 +512,21 @@
 
             @pl.when(r == 0)
             def _():
-                tail(k)
-
-            prompt(i, k, r)
+                tail(k, ((i // thirds) % 2) * thirds)
+
+            prompt(i)
+            kept = ((i // thirds) % 2) * thirds + r
+            store(i, 0, out_a, top_a, tail_out.at[kept], tail_stat.at[kept])
+
+        @pl.when(i == units)
+        def _():
+            prompt_last()
 
         for late in reversed(range(len(stages))):
 
-            @pl.when((i >= late) & (i < units + late))
+            @pl.when((i > late) & (i <= units + late))
             def _(late=late):
-                stages[late](i - late)
+                stages[late](i - late - 1)
 
         for at_turn, calls in q_hooks.items():
 
@@ -497,9 +537,9 @@
 
         return carry
 
-    lax.fori_loop(0, units + len(stages) - 1, turn, 0)
-    for r in range(thirds):
-        swap(r).wait()
+    lax.fori_loop(0, units + len(stages), turn, 0)
+    swap().start()
+    swap().wait()
     out[...] = (total[pl.ds(2 * head, 2)] + x_part[...]).reshape(out.shape)
 
 
@@ -545,8 +585,16 @@
             pltpu.VMEM((rows, width), f32),
             pltpu.VMEM((rows, tail_len), f32),
             pltpu.VMEM((rows, width), f32),
-            pltpu.VMEM((thirds, ZS, width, lanes), f32),
-            pltpu.VMEM((thirds, ZS, 8, lanes), f32),
+            pltpu.VMEM((2 * thirds, ZS, width, lanes), f32),
+            pltpu.VMEM((2 * thirds, ZS, 8, lanes), f32),
+            pltpu.VMEM((positions, 2 * lanes), f32),
+            pltpu.VMEM((positions, 2 * lanes), f32),
+            pltpu.VMEM((positions, 2 * lanes), bf16),
+            pltpu.VMEM((width + 16, 2 * lanes), f32),
+            pltpu.VMEM((width + 16, 2 * lanes), f32),
+            pltpu.VMEM((8, 2 * lanes), f32),
+            pltpu.VMEM((8, 2 * lanes), f32),
+            pltpu.VMEM((8, 2 * lanes), f32),
             pltpu.VMEM((units, YS, CS, width, lanes), bf16),
             pltpu.VMEM((units, YS, CS, 8, lanes), f32),
             pltpu.VMEM((units, YS, width, lanes), bf16),
@@ -576,7 +624,7 @@
             sem((units, ZS - 1)),
             sem((units,)),
             sem((units, 4)),
-            sem((thirds, 2)),
+            sem((2,)),
         ],
         compiler_params=pltpu.CompilerParams(
             collective_id=0, has_side_effects=True, vmem_limit_bytes=62 * 1024 * 1024

time: 93.2 us -> 101 us (1.084)
  Pallas kernels: 91.5 us -> 98.8 us
    pallas_call x1, Pallas kernels: 91.5 us -> 98.8 us  [fused(): pl.pallas_call(functools.partial(kernel, unit), out_shape=jax.ShapeDtypeS...]
where the time goes in v4:
time: 101 us; the launch traced here: 100 us
  Pallas kernels  98.8 us (98%)
  local copies, waits for them, and re-layouts  1.58 us (2%)
    pallas_call x1, Pallas kernels, fused(): pl.pallas_call(functools.partial(kernel, unit), out_shape=jax.ShapeDtypeS...  98.8 us

profile of v4, /device:TPU:0, one launch (start us, length us, event | category | flops | bytes accessed | tf_op | source)
XLA Modules:
  0.0 100.3 jit_solution(9593306538321784110)
XLA Ops:
  0.0 98.8 %shard_map.82 = f32[96,320]{1,0:T(8,128)} custom-call(bf16[12,32,128]{2,1,0:T(8,128)(2,1)} %q_in.1, bf16[8192,128]{1,0:T(8,128)(2,1)} %bitcast.5, bf16[8192,128]{1,0:T(8,128)(2,1)} %bitcast.6, bf16[12,4,1024,128]{3,2,1,0:T(8,128)(2,1)} %tail_keys_in.1, bf16[12,4,1024,128]{3,2,1,0:T(8,128)(2,1)} %tail_values_in.1, s32[12]{0:T(128)} %lengths.1, ...), custom_call_target="tpu_custom_call" | custom-call | tf_op jit(solution)/shard_map/pallas_call | solution.py:568
  98.8 1.6 %copy.10 = f32[96,320]{1,0:T(8,128)} copy(f32[96,320]{1,0:T(8,128)} %shard_map.82) | data formatting | bytes 245760

commit v5 on v3

--- a/solution.py
+++ b/solution.py
@@ -60,14 +60,9 @@
     tail_stat,
     part,
     stat,
-    core_part,
-    core_stat,
-    y_own,
-    y_send,
-    y_part,
-    y_own_stat,
-    y_send_stat,
-    y_stat,
+    near_part,
+    near_stat,
+    z_own,
     z_send,
     z_send_stat,
     z_part,
@@ -77,16 +72,11 @@
     x_part,
     load_sem,
     tail_sem,
-    q_sems,
-    qz_send_sem,
-    qz_recv_sem,
-    core_sems,
-    y_sems,
-    zs_send,
-    zs_recv,
-    az_send,
-    az_recv,
-    a_sems,
+    qz_sems,
+    qn_sems,
+    near_sems,
+    z_sems,
+    att_sems,
     x_sems,
 ):
     kv_count, rows_local, width = q_own.shape
@@ -99,13 +89,15 @@
     units = kv_count * thirds
     seq, head = lax.axis_index("seq"), lax.axis_index("head")
     z, y, core = seq // (YS * CS), (seq // CS) % YS, seq % CS
-    other_y, other_core, other_head = 1 - y, 1 - core, 1 - head
+    other_head = 1 - head
 
     def at(z_to, y_to, core_to):
         return ((z_to * YS + y_to) * CS + core_to, head)
 
     z_peers = [at((z + step) % ZS, y, core) for step in range(1, ZS)]
-    y_peer, core_peer, x_peer = at(z, other_y, core), at(z, y, other_core), (seq, other_head)
+    near = [((y + step // CS) % YS, (core + step % CS) % CS) for step in range(1, YS * CS)]
+    near_peers = [at(z, *place) for place in near]
+    x_peer = (seq, other_head)
     order = [(3 * turn) % kv_count for turn in range(kv_count)]
 
     def remote(source, target, send, recv, device):
@@ -145,7 +137,7 @@
         q_own[k] = dot(onehot(grid(shape, 1) == place + k * group), flat, NN).astype(jnp.bfloat16)
 
     barrier = pltpu.get_barrier_semaphore()
-    peers = z_peers + [y_peer, core_peer, x_peer]
+    peers = z_peers + near_peers + [x_peer]
     for peer in peers:
         pl.semaphore_signal(barrier, inc=1, device_id=peer, device_id_type=MESH)
     pl.semaphore_wait(barrier, len(peers))
@@ -155,45 +147,36 @@
 
     def q_z(k):
         return [
-            remote(q_own.at[k], q_all.at[k, z, block(y, core)], qz_send_sem.at[k, i], qz_recv_sem.at[k, i], z_peers[i])
+            remote(
+                q_own.at[k], q_all.at[k, z, block(y, core)], qz_sems.at[k, i, 0], qz_sems.at[k, i, 1], z_peers[i]
+            )
             for i in range(ZS - 1)
         ]
 
-    def q_y(k):
+    def q_near(k):
         mine = q_all.at[k, :, block(y, core)]
-        return remote(mine, mine, q_sems.at[k, 0], q_sems.at[k, 1], y_peer)
-
-    def q_core(k):
         return [
-            remote(
-                q_all.at[k, :, block(i, core)],
-                q_all.at[k, :, block(i, core)],
-                q_sems.at[k, 2 + 2 * i],
-                q_sems.at[k, 3 + 2 * i],
-                core_peer,
-            )
-            for i in range(YS)
+            remote(mine, mine, qn_sems.at[k, i, 0], qn_sems.at[k, i, 1], near_peers[i]) for i in range(YS * CS - 1)
         ]
 
-    for k in order:
-        for copy in q_z(k):
+    def start(copies):
+        for copy in copies:
             copy.start()
+
+    def wait(copies):
+        for copy in copies:
+            copy.wait()
+
+    start(q_z(order[0]))
     for k in order:
         q_all[k, z, block(y, core), :] = q_own[k]
 
     def q_after_z(k):
-        for copy in q_z(k):
-            copy.wait()
-        q_y(k).start()
-
-    def q_after_y(k):
-        q_y(k).wait()
-        for copy in q_core(k):
-            copy.start()
+        wait(q_z(k))
+        start(q_near(k))
 
     def q_ready(k):
-        for copy in q_core(k):
-            copy.wait()
+        wait(q_near(k))
 
     def split_keys():
         size = 256 // kv_count
@@ -287,151 +270,86 @@
                 stat[u, p, c, 0:1] = m
                 stat[u, p, c, 1:2] = l
 
-    def sum_core(u):
-        return [
-            remote(part.at[u, :, other_core], core_part.at[u], core_sems.at[u, 0], core_sems.at[u, 1], core_peer),
-            remote(stat.at[u, :, other_core], core_stat.at[u], core_sems.at[u, 2], core_sems.at[u, 3], core_peer),
-        ]
-
-    def sum_y(u):
-        return [
-            remote(y_send.at[u], y_part.at[u], y_sems.at[u, 0], y_sems.at[u, 1], y_peer),
-            remote(y_send_stat.at[u], y_stat.at[u], y_sems.at[u, 2], y_sems.at[u, 3], y_peer),
-        ]
-
     def head_of(u):
         return (3 * (u // thirds)) % kv_count
 
-    def sum_z_out(u):
-        k, r = head_of(u), u % thirds
-        slot = (z - k + 2 * ZS - 1) % ZS
+    def sum_near(u):
+        copies = []
+        for i, (y_to, core_to) in enumerate(near):
+            sems = near_sems.at[u, i]
+            copies += [
+                remote(part.at[u, y_to, core_to], near_part.at[u, i], sems.at[0], sems.at[1], near_peers[i]),
+                remote(stat.at[u, y_to, core_to], near_stat.at[u, i], sems.at[2], sems.at[3], near_peers[i]),
+            ]
+        return copies
+
+    def sum_z(u):
+        copies = []
+        for i in range(ZS - 1):
+            sems = z_sems.at[u, i]
+            copies += [
+                remote(z_send.at[u], z_part.at[u, i], sems.at[0], sems.at[1], z_peers[i]),
+                remote(z_send_stat.at[u], z_stat.at[u, i], sems.at[2], sems.at[3], z_peers[i]),
+            ]
+        return copies
+
+    def att_near(u):
+        mine = att.at[u, y, core]
         return [
-            remote(z_send.at[u], z_part.at[r, slot], zs_send.at[u, 0], zs_recv.at[r, slot, 0], at(k, y, core)),
-            remote(z_send_stat.at[u], z_stat.at[r, slot], zs_send.at[u, 1], zs_recv.at[r, slot, 1], at(k, y, core)),
+            remote(mine, mine, att_sems.at[u, i, 0], att_sems.at[u, i, 1], near_peers[i]) for i in range(YS * CS - 1)
         ]
 
-    def sum_z_in(u, slot):
-        r = u % thirds
-        return [
-            remote(z_send.at[u], z_part.at[r, slot], zs_send.at[u, 0], zs_recv.at[r, slot, 0], y_peer),
-            remote(z_send_stat.at[u], z_stat.at[r, slot], zs_send.at[u, 1], zs_recv.at[r, slot, 1], y_peer),
-        ]
-
-    def att_z(u, i):
-        mine = att.at[u, y, core]
-        return remote(mine, mine, az_send.at[u, i], az_recv.at[u], z_peers[i])
-
-    def att_y(u):
-        mine = att.at[u, y, core]
-        return remote(mine, mine, a_sems.at[u, 0], a_sems.at[u, 1], y_peer)
-
-    def att_core(u):
-        mine = att.at[u, :, core]
-        return remote(mine, mine, a_sems.at[u, 2], a_sems.at[u, 3], core_peer)
-
-    def swap(r):
-        rows = pl.ds(r * (lanes // group), lanes // group)
-        return remote(
-            total.at[pl.ds(2 * other_head, 2), rows],
-            x_part.at[:, rows],
-            x_sems.at[r, 0],
-            x_sems.at[r, 1],
-            x_peer,
-        )
+    def swap():
+        return remote(total.at[pl.ds(2 * other_head, 2)], x_part, x_sems.at[0], x_sems.at[1], x_peer)
 
     def step_a(u):
-        for copy in sum_core(u):
-            copy.start()
+        start(sum_near(u))
 
     def step_b(u):
-        for copy in sum_core(u):
-            copy.wait()
-
-        def joined(i):
-            return merge(
-                [
-                    (part[u, i, core].astype(jnp.float32), stat[u, i, core, 0:1], stat[u, i, core, 1:2]),
-                    (core_part[u, i].astype(jnp.float32), core_stat[u, i, 0:1], core_stat[u, i, 1:2]),
-                ],
-                unit,
-            )
-
-        o, m, l = joined(other_y)
-        y_send[u] = o.astype(jnp.bfloat16)
-        y_send_stat[u, 0:1] = m
-        y_send_stat[u, 1:2] = l
-        for copy in sum_y(u):
-            copy.start()
-        o, m, l = joined(y)
-        y_own[u] = o
-        y_own_stat[u, 0:1] = m
-        y_own_stat[u, 1:2] = l
-
-    def step_c(u):
-        for copy in sum_y(u):
-            copy.wait()
-        o, m, l = merge(
-            [
-                (y_own[u], y_own_stat[u, 0:1], y_own_stat[u, 1:2]),
-                (y_part[u].astype(jnp.float32), y_stat[u, 0:1], y_stat[u, 1:2]),
-            ],
-            unit,
-        )
-        y_own[u] = o
+        wait(sum_near(u))
+        parts = [(part[u, y, core].astype(jnp.float32), stat[u, y, core, 0:1], stat[u, y, core, 1:2])]
+        for i in range(YS * CS - 1):
+            parts.append((near_part[u, i].astype(jnp.float32), near_stat[u, i, 0:1], near_stat[u, i, 1:2]))
+        o, m, l = merge(parts, unit)
+        z_own[u] = o
         z_send[u] = o.astype(jnp.bfloat16)
         z_send_stat[u, 0:1] = m
         z_send_stat[u, 1:2] = l
-
-        @pl.when(z != head_of(u))
+        start(sum_z(u))
+
+    def step_c(u):
+        wait(sum_z(u))
+        parts = [(z_own[u], z_send_stat[u, 0:1], z_send_stat[u, 1:2])]
+        for i in range(ZS - 1):
+            parts.append((z_part[u, i].astype(jnp.float32), z_stat[u, i, 0:1], z_stat[u, i, 1:2]))
+        o, _, l = merge(parts, unit)
+        attention = (o / l).astype(jnp.bfloat16)
+        rows = dot(perm[...], attention, NT).astype(jnp.bfloat16)
+        att[u, y, core] = rows.reshape(att.shape[3:])
+        start(att_near(u))
+
+    def step_d(u):
+        wait(att_near(u))
+
+        @pl.when(u % thirds == thirds - 1)
         def _():
-            for copy in sum_z_out(u):
-                copy.start()
-
-    def step_d(u):
-        @pl.when(z != head_of(u))
-        def _():
-            for copy in sum_z_out(u):
-                copy.wait_send()
-
-        @pl.when(z == head_of(u))
-        def _():
-            parts = [(y_own[u], z_send_stat[u, 0:1], z_send_stat[u, 1:2])]
-            r = u % thirds
-            for slot in range(ZS - 1):
-                for copy in sum_z_in(u, slot):
-                    copy.wait_recv()
-                parts.append((z_part[r, slot].astype(jnp.float32), z_stat[r, slot, 0:1], z_stat[r, slot, 1:2]))
-            o, _, l = merge(parts, unit)
-            attention = (o / l).astype(jnp.bfloat16)
-            rows = dot(perm[...], attention, NT).astype(jnp.bfloat16)
-            att[u, y, core] = rows.reshape(att.shape[3:])
-            for i in range(ZS - 1):
-                att_z(u, i).start()
-
-    def step_e(u):
-        @pl.when(z != head_of(u))
-        def _():
-            att_z(u, 0).wait_recv()
-
-        att_y(u).start()
-
-    def step_f(u):
-        @pl.when(z == head_of(u))
-        def _():
-            for i in range(ZS - 1):
-                att_z(u, i).wait_send()
-
-        att_y(u).wait()
-        att_core(u).start()
-
-    def step_g(u):
-        att_core(u).wait()
-        k, r = head_of(u), u % thirds
+            project(u // thirds)
+
+    def project(turn_of):
+        k = (3 * turn_of) % kv_count
         value = None
         for g in range(0, group, 2):
             rows = jnp.concatenate(
                 [
-                    jnp.concatenate([att[u, i, j, g + h] for i in range(YS) for j in range(CS)], axis=0)
+                    jnp.concatenate(
+                        [
+                            att[turn_of * thirds + r, i, j, g + h]
+                            for i in range(YS)
+                            for j in range(CS)
+                            for r in range(thirds)
+                        ],
+                        axis=0,
+                    )
                     for h in range(2)
                 ],
                 axis=1,
@@ -439,37 +357,29 @@
             first = pl.multiple_of((k * group + g) * width, 2 * width)
             term = dot(rows, weight[:, pl.ds(first, 2 * width)], NT)
             value = term if value is None else value + term
-        count = lanes // group
-        rows = pl.ds(pl.multiple_of(r * count, count), count)
-        for c in range(ZS):
-            total[c, rows, :] += value[c * count : (c + 1) * count]
-
-        @pl.when(u >= units - thirds)
-        def _():
-            swap(r).start()
+        total[...] += value.reshape(total.shape)
 
     a, b, c, d = order
     prepare()
+    for k in order[1:]:
+        start(q_z(k))
     loads[0].wait()
     split_keys()
     q_after_z(a)
     loads[1].wait()
     split_values()
-    q_after_y(a)
     q_after_z(b)
     q_ready(a)
-
     total[...] = jnp.zeros_like(total)
     loads[2].wait()
     q_hooks = {
-        0: [(q_after_z, c), (q_after_y, b)],
+        0: [(q_after_z, c)],
         1: [(q_after_z, d)],
-        2: [(q_ready, b), (q_after_y, c)],
-        3: [(q_after_y, d)],
+        2: [(q_ready, b)],
         5: [(q_ready, c)],
         8: [(q_ready, d)],
     }
-    stages = [step_a, step_b, step_c, step_d, step_e, step_f, step_g]
+    stages = [step_a, step_b, step_c, step_d]
 
     def turn(i, carry):
         @pl.when(i < units)
@@ -498,8 +408,8 @@
         return carry
 
     lax.fori_loop(0, units + len(stages) - 1, turn, 0)
-    for r in range(thirds):
-        swap(r).wait()
+    swap().start()
+    swap().wait()
     out[...] = (total[pl.ds(2 * head, 2)] + x_part[...]).reshape(out.shape)
 
 
@@ -549,34 +459,24 @@
             pltpu.VMEM((thirds, ZS, 8, lanes), f32),
             pltpu.VMEM((units, YS, CS, width, lanes), bf16),
             pltpu.VMEM((units, YS, CS, 8, lanes), f32),
-            pltpu.VMEM((units, YS, width, lanes), bf16),
-            pltpu.VMEM((units, YS, 8, lanes), f32),
+            pltpu.VMEM((units, YS * CS - 1, width, lanes), bf16),
+            pltpu.VMEM((units, YS * CS - 1, 8, lanes), f32),
             pltpu.VMEM((units, width, lanes), f32),
             pltpu.VMEM((units, width, lanes), bf16),
-            pltpu.VMEM((units, width, lanes), bf16),
             pltpu.VMEM((units, 8, lanes), f32),
-            pltpu.VMEM((units, 8, lanes), f32),
-            pltpu.VMEM((units, 8, lanes), f32),
-            pltpu.VMEM((units, width, lanes), bf16),
-            pltpu.VMEM((units, 8, lanes), f32),
-            pltpu.VMEM((thirds, ZS - 1, width, lanes), bf16),
-            pltpu.VMEM((thirds, ZS - 1, 8, lanes), f32),
+            pltpu.VMEM((units, ZS - 1, width, lanes), bf16),
+            pltpu.VMEM((units, ZS - 1, 8, lanes), f32),
             pltpu.VMEM((units, YS, CS, group, lanes // group, width), bf16),
             pltpu.VMEM((ZS, samples // ZS, out_columns), f32),
             pltpu.VMEM((2, samples // ZS, out_columns), f32),
             sem((3,)),
             sem((kv, 2)),
-            sem((kv, 6)),
-            sem((kv, ZS - 1)),
-            sem((kv, ZS - 1)),
-            sem((units, 4)),
-            sem((units, 4)),
-            sem((units, 2)),
-            sem((thirds, ZS - 1, 2)),
-            sem((units, ZS - 1)),
-            sem((units,)),
-            sem((units, 4)),
-            sem((thirds, 2)),
+            sem((kv, ZS - 1, 2)),
+            sem((kv, YS * CS - 1, 2)),
+            sem((units, YS * CS - 1, 4)),
+            sem((units, ZS - 1, 4)),
+            sem((units, YS * CS - 1, 2)),
+            sem((2,)),
         ],
         compiler_params=pltpu.CompilerParams(
             collective_id=0, has_side_effects=True, vmem_limit_bytes=62 * 1024 * 1024

time: 93.2 us -> 102 us (1.094)
  Pallas kernels: 91.5 us -> 100 us
    pallas_call x1, Pallas kernels: 91.5 us -> 100 us  [fused(): pl.pallas_call(functools.partial(kernel, unit), out_shape=jax.ShapeDtypeS...]
where the time goes in v5:
time: 102 us
  Pallas kernels  100 us (98%)
  local copies, waits for them, and re-layouts  1.58 us (2%)
    pallas_call x1, Pallas kernels, fused(): pl.pallas_call(functools.partial(kernel, unit), out_shape=jax.ShapeDtypeS...  100 us

profile of v5, /device:TPU:0, one launch (start us, length us, event | category | flops | bytes accessed | tf_op | source)
XLA Modules:
  0.0 101.9 jit_solution(1009139435837391335)
XLA Ops:
  0.0 100.3 %shard_map.82 = f32[96,320]{1,0:T(8,128)} custom-call(bf16[12,32,128]{2,1,0:T(8,128)(2,1)} %q_in.1, bf16[8192,128]{1,0:T(8,128)(2,1)} %bitcast.5, bf16[8192,128]{1,0:T(8,128)(2,1)} %bitcast.6, bf16[12,4,1024,128]{3,2,1,0:T(8,128)(2,1)} %tail_keys_in.1, bf16[12,4,1024,128]{3,2,1,0:T(8,128)(2,1)} %tail_values_in.1, s32[12]{0:T(128)} %lengths.1, ...), custom_call_target="tpu_custom_call" | custom-call | tf_op jit(solution)/shard_map/pallas_call | solution.py:438
  100.3 1.6 %copy.10 = f32[96,320]{1,0:T(8,128)} copy(f32[96,320]{1,0:T(8,128)} %shard_map.82) | data formatting | bytes 245760

commit v6 on v2

--- a/solution.py
+++ b/solution.py
@@ -162,9 +162,11 @@
         mine = q_all.at[k, :, :, core]
         return remote(mine, mine, q_sems.at[k, 2], q_sems.at[k, 3], core_peer)
 
-    for k in order:
+    def q_start(k):
         for copy in q_z(k):
             copy.start()
+
+    q_start(order[0])
     for k in order:
         q_all[k, z, y, core] = q_own[k]
 
@@ -247,10 +249,18 @@
 
     def prompt(k, pair):
         q = q_all[k, pl.ds(pair * 2, 2)].reshape(2 * chunk, width)
-        scores = dot(keys[k], q, NT)
-        top = jnp.max(scores, axis=0, keepdims=True)
-        weights = jnp.exp2((scores - top) * unit)
-        both = dot(values[k], weights.astype(jnp.bfloat16), NN)
+        wide = 256
+        count = 2 * chunk // wide
+        scores = [dot(keys[k], q[:wide], NT)]
+        tops, boths = [], []
+        for j in range(count):
+            if j + 1 < count:
+                scores.append(dot(keys[k], q[(j + 1) * wide : (j + 2) * wide], NT))
+            top = jnp.max(scores[j], axis=0, keepdims=True)
+            weights = jnp.exp2((scores[j] - top) * unit).astype(jnp.bfloat16)
+            tops.append(top)
+            boths.append(dot(values[k], weights, NN))
+        top, both = jnp.concatenate(tops, axis=1), jnp.concatenate(boths, axis=1)
         rows, count = both[:width], both[width : width + 1]
         for c in range(2):
             span = slice(c * chunk, (c + 1) * chunk)
@@ -398,65 +408,72 @@
             first = (k * group + g) * width
             term = dot(block, weight[:, first : first + 2 * width], NT)
             value = term if value is None else value + term
-        return value
+        half = value.shape[0] // 2
+        total[0] += value[:half]
+        total[1] += value[half:]
 
     a, b, c, d = order
     prepare()
     loads[0].wait()
     split_keys()
     q_after_z(a)
+    q_start(b)
     loads[1].wait()
     split_values()
     q_after_y(a)
-    q_after_z(b)
+    q_start(c)
+    q_start(d)
+    loads[2].wait()
+    total[...] = jnp.zeros_like(total)
     q_ready(a)
 
+    mid_hooks = {
+        0: [(q_after_z, b)],
+        2: [(step_b, a), (q_after_y, c)],
+        4: [(step_e, a), (step_b, b)],
+        6: [(step_e, b), (step_b, c)],
+    }
     hooks = {
-        0: [(q_after_z, c), (q_after_y, b)],
-        1: [(step_a, a), (q_after_z, d), (q_after_y, c), (q_ready, b)],
-        2: [(step_b, a), (q_after_y, d)],
-        3: [(step_c, a), (step_a, b), (q_ready, c)],
-        4: [(step_d, a), (step_b, b)],
-        5: [(step_e, a), (step_c, b), (step_a, c), (q_ready, d)],
-        6: [(step_f, a), (step_d, b), (step_b, c)],
-        7: [(step_a, d), (step_e, b), (step_c, c)],
+        0: [(q_after_y, b), (q_after_z, c)],
+        1: [(step_a, a), (q_ready, b), (q_after_z, d)],
+        2: [(step_c, a), (q_after_y, d)],
+        3: [(step_d, a), (step_a, b), (q_ready, c)],
+        4: [(step_f, a), (step_c, b)],
+        5: [(step_a, c), (step_g, a), (step_d, b), (q_ready, d)],
+        6: [(step_f, b), (step_c, c)],
+        7: [(step_a, d), (step_g, b), (step_d, c)],
     }
 
-    def turn(i, carry):
-        k, pair = (3 * (i // 2)) % kv_count, i % 2
-
-        @pl.when(pair == 0)
-        def _():
-            tail(k)
-
-        prompt(k, pair)
-        for at_turn, calls in hooks.items():
+    def run(i, table):
+        for at_turn, calls in table.items():
 
             @pl.when(i == at_turn)
             def _(calls=calls):
                 for call, at_k in calls:
                     call(at_k)
 
+    def turn(i, carry):
+        k, pair = (3 * (i // 2)) % kv_count, i % 2
+
+        @pl.when(pair == 0)
+        def _():
+            tail(k)
+            run(i, mid_hooks)
+
+        prompt(k, pair)
+        run(i, hooks)
         return carry
 
     lax.fori_loop(0, 2 * kv_count, turn, 0)
     step_b(d)
-    step_d(c)
-    step_f(b)
+    step_e(c)
     step_c(d)
-    loads[2].wait()
-    value = step_g(a)
-    step_e(c)
+    step_f(c)
     step_d(d)
-    value += step_g(b)
-    step_f(c)
+    step_g(c)
     step_e(d)
-    value += step_g(c)
     step_f(d)
-    value += step_g(d)
-    half = value.shape[0] // 2
-    total[0] = value[:half]
-    total[1] = value[half:]
+    step_g(d)
     swap = remote(total.at[other_head], x_part, x_sems.at[0], x_sems.at[1], x_peer)
     swap.start()
     swap.wait()

time: 92.6 us -> 101 us (1.091)
  Pallas kernels: 90.9 us -> 98.8 us
    pallas_call x1, Pallas kernels: 90.9 us -> 98.8 us  [fused(): pl.pallas_call(functools.partial(kernel, unit), out_shape=jax.ShapeDtypeS...]
where the time goes in v6:
time: 101 us; the launch traced here: 100 us
  Pallas kernels  98.8 us (98%)
  local copies, waits for them, and re-layouts  1.58 us (2%)
    pallas_call x1, Pallas kernels, fused(): pl.pallas_call(functools.partial(kernel, unit), out_shape=jax.ShapeDtypeS...  98.8 us

profile of v6, /device:TPU:0, one launch (start us, length us, event | category | flops | bytes accessed | tf_op | source)
XLA Modules:
  0.0 100.4 jit_solution(13623818000540312662)
XLA Ops:
  0.0 98.8 %shard_map.82 = f32[96,320]{1,0:T(8,128)} custom-call(bf16[12,32,128]{2,1,0:T(8,128)(2,1)} %q_in.1, bf16[8192,128]{1,0:T(8,128)(2,1)} %bitcast.5, bf16[8192,128]{1,0:T(8,128)(2,1)} %bitcast.6, bf16[12,4,1024,128]{3,2,1,0:T(8,128)(2,1)} %tail_keys_in.1, bf16[12,4,1024,128]{3,2,1,0:T(8,128)(2,1)} %tail_values_in.1, s32[12]{0:T(128)} %lengths.1, ...), custom_call_target="tpu_custom_call" | custom-call | tf_op jit(solution)/shard_map/pallas_call | solution.py:503
  98.8 1.6 %copy.10 = f32[96,320]{1,0:T(8,128)} copy(f32[96,320]{1,0:T(8,128)} %shard_map.82) | data formatting | bytes 245760

commit v7 on v3

--- a/solution.py
+++ b/solution.py
@@ -267,25 +267,22 @@
 
     def prompt(u, k, r):
         q = q_all[k, :, pl.ds(pl.multiple_of(r * lanes, lanes), lanes), :]
-        pairs = ZS // 2
-        scores = [dot(keys[k], q[2 * p : 2 * p + 2].reshape(2 * lanes, width), NT) for p in range(pairs)]
-        for p in range(pairs):
-            top = jnp.max(scores[p], axis=0, keepdims=True)
-            weights = jnp.exp2((scores[p] - top) * unit).astype(jnp.bfloat16)
-            both = dot(values[k], weights, NN)
-            for c in range(2):
-                span = slice(c * lanes, (c + 1) * lanes)
-                at_chunk = p * 2 + c
-                o, m, l = merge(
-                    [
-                        (both[:width, span], top[:, span], both[width : width + 1, span]),
-                        (tail_out[r, at_chunk], tail_stat[r, at_chunk, 0:1], tail_stat[r, at_chunk, 1:2]),
-                    ],
-                    unit,
-                )
-                part[u, p, c] = o.astype(jnp.bfloat16)
-                stat[u, p, c, 0:1] = m
-                stat[u, p, c, 1:2] = l
+        scores = dot(keys[k], q.reshape(ZS * lanes, width), NT)
+        top = jnp.max(scores, axis=0, keepdims=True)
+        weights = jnp.exp2((scores - top) * unit).astype(jnp.bfloat16)
+        both = dot(values[k], weights, NN)
+        for c in range(ZS):
+            span = slice(c * lanes, (c + 1) * lanes)
+            o, m, l = merge(
+                [
+                    (both[:width, span], top[:, span], both[width : width + 1, span]),
+                    (tail_out[r, c], tail_stat[r, c, 0:1], tail_stat[r, c, 1:2]),
+                ],
+                unit,
+            )
+            part[u, c // CS, c % CS] = o.astype(jnp.bfloat16)
+            stat[u, c // CS, c % CS, 0:1] = m
+            stat[u, c // CS, c % CS, 1:2] = l
 
     def sum_core(u):
         return [
@@ -329,15 +326,8 @@
         mine = att.at[u, :, core]
         return remote(mine, mine, a_sems.at[u, 2], a_sems.at[u, 3], core_peer)
 
-    def swap(r):
-        rows = pl.ds(r * (lanes // group), lanes // group)
-        return remote(
-            total.at[pl.ds(2 * other_head, 2), rows],
-            x_part.at[:, rows],
-            x_sems.at[r, 0],
-            x_sems.at[r, 1],
-            x_peer,
-        )
+    def swap():
+        return remote(total.at[pl.ds(2 * other_head, 2)], x_part, x_sems.at[0], x_sems.at[1], x_peer)
 
     def step_a(u):
         for copy in sum_core(u):
@@ -426,12 +416,26 @@
 
     def step_g(u):
         att_core(u).wait()
-        k, r = head_of(u), u % thirds
+
+        @pl.when(u % thirds == thirds - 1)
+        def _():
+            project(u // thirds)
+
+    def project(turn_of):
+        k = (3 * turn_of) % kv_count
         value = None
         for g in range(0, group, 2):
             rows = jnp.concatenate(
                 [
-                    jnp.concatenate([att[u, i, j, g + h] for i in range(YS) for j in range(CS)], axis=0)
+                    jnp.concatenate(
+                        [
+                            att[turn_of * thirds + r, i, j, g + h]
+                            for i in range(YS)
+                            for j in range(CS)
+                            for r in range(thirds)
+                        ],
+                        axis=0,
+                    )
                     for h in range(2)
                 ],
                 axis=1,
@@ -439,14 +443,7 @@
             first = pl.multiple_of((k * group + g) * width, 2 * width)
             term = dot(rows, weight[:, pl.ds(first, 2 * width)], NT)
             value = term if value is None else value + term
-        count = lanes // group
-        rows = pl.ds(pl.multiple_of(r * count, count), count)
-        for c in range(ZS):
-            total[c, rows, :] += value[c * count : (c + 1) * count]
-
-        @pl.when(u >= units - thirds)
-        def _():
-            swap(r).start()
+        total[...] += value.reshape(total.shape)
 
     a, b, c, d = order
     prepare()
@@ -498,8 +495,8 @@
         return carry
 
     lax.fori_loop(0, units + len(stages) - 1, turn, 0)
-    for r in range(thirds):
-        swap(r).wait()
+    swap().start()
+    swap().wait()
     out[...] = (total[pl.ds(2 * head, 2)] + x_part[...]).reshape(out.shape)
 
 
@@ -576,7 +573,7 @@
             sem((units, ZS - 1)),
             sem((units,)),
             sem((units, 4)),
-            sem((thirds, 2)),
+            sem((2,)),
         ],
         compiler_params=pltpu.CompilerParams(
             collective_id=0, has_side_effects=True, vmem_limit_bytes=62 * 1024 * 1024

time: 93.2 us -> 95 us (1.019)
  Pallas kernels: 91.5 us -> 93.3 us
    pallas_call x1, Pallas kernels: 91.5 us -> 93.3 us  [fused(): pl.pallas_call(functools.partial(kernel, unit), out_shape=jax.ShapeDtypeS...]
where the time goes in v7:
time: 95 us; the launch traced here: 94.9 us
  Pallas kernels  93.3 us (98%)
  local copies, waits for them, and re-layouts  1.58 us (2%)
    pallas_call x1, Pallas kernels, fused(): pl.pallas_call(functools.partial(kernel, unit), out_shape=jax.ShapeDtypeS...  93.3 us

profile of v7, /device:TPU:0, one launch (start us, length us, event | category | flops | bytes accessed | tf_op | source)
XLA Modules:
  0.0 94.9 jit_solution(6496593259416716422)
XLA Ops:
  0.0 93.3 %shard_map.82 = f32[96,320]{1,0:T(8,128)} custom-call(bf16[12,32,128]{2,1,0:T(8,128)(2,1)} %q_in.1, bf16[8192,128]{1,0:T(8,128)(2,1)} %bitcast.5, bf16[8192,128]{1,0:T(8,128)(2,1)} %bitcast.6, bf16[12,4,1024,128]{3,2,1,0:T(8,128)(2,1)} %tail_keys_in.1, bf16[12,4,1024,128]{3,2,1,0:T(8,128)(2,1)} %tail_values_in.1, s32[12]{0:T(128)} %lengths.1, ...), custom_call_target="tpu_custom_call" | custom-call | tf_op jit(solution)/shard_map/pallas_call | solution.py:525
  93.3 1.6 %copy.10 = f32[96,320]{1,0:T(8,128)} copy(f32[96,320]{1,0:T(8,128)} %shard_map.82) | data formatting | bytes 245760
